TPU v7x, 512 devices: a whole 4x4x16 slice. The times are simulated.
512 devices in a mesh: gx: 32 (over x_hi, z), gy: 16 (over x_lo, y, core).
Axes of the slice: x: 4 (x_hi: 2, x_lo: 2; x = x_hi * 2 + x_lo), y: 4, z: 16, core: 2. Of those that a mesh axis runs over, the one named last changes fastest.
Arguments:
- matrix: float32 [262144, 512], P(('gx', 'gy'))
- signs: int32 [262144], P(('gx', 'gy')), may hold values from -1 to 1, as said below
- samples: int32 [2048], replicated, may hold values from 0 to 262143, as said below
Outputs:
- factor: float32 [512, 512], replicated
- preconditioned: float32 [262144, 512], P(('gx', 'gy'))
Inputs may be any that keep to these rules, and one draw needn't show every extreme that they name: `signs`: each entry is +1 or -1. `samples`: row indices drawn with replacement; may repeat.
All inputs are finite; a program needn't handle non-finite values.
Results may differ from a plain program's by a relative error of at most 0.00012.
Values sent between devices are 32-bit elements; how exact they have to be, the bound alone decides.
No kernel may reach another device: no remote copies, remote signals or barrier semaphores. Data moves between devices by JAX's collectives and lax.ppermute only.
A program may use at most 64 MiB of HBM per device.

v0:
```python
import jax
import jax.numpy as jnp
from jax import lax
from jax.sharding import PartitionSpec as P


def partner_2(block, axis, stride):
    count = lax.axis_size(axis)
    route = []
    for low in range(count):
        high = low | 1 << stride
        if high != low and high < count:
            route += [(low, high), (high, low)]
    return lax.ppermute(block, axis, route)


def bit_parity(value, nbits):
    parity = jnp.zeros_like(value)
    for bit in range(nbits):
        parity = parity ^ value >> bit & 1
    return parity


def hadamard_table(count):
    positions = jnp.arange(count, dtype=jnp.int32)
    parity = bit_parity(positions[:, None] & positions[None, :], count.bit_length())
    return (1 - 2 * parity).astype(jnp.float32)


def owner_gram(mixed, samples, local_rows, device):
    owner = samples // local_rows
    within = samples % local_rows
    positions = jnp.arange(local_rows, dtype=jnp.int32)
    hits = (owner[:, None] == device) & (within[:, None] == positions[None, :])
    tally = jnp.sum(hits.astype(jnp.float32), axis=0)
    return jnp.dot((mixed * tally[:, None]).T, mixed, precision=lax.Precision.HIGHEST)


def body(matrix, signs, samples):
    local_rows = matrix.shape[0]
    count_gx = lax.axis_size("gx")
    count_gy = lax.axis_size("gy")
    devices = count_gx * count_gy
    total_rows = local_rows * devices
    signed = signs.astype(jnp.float32)[:, None] * matrix
    local_mix = jnp.dot(hadamard_table(local_rows), signed, precision=lax.Precision.HIGHEST)
    local_mix = local_mix / jnp.sqrt(jnp.float32(total_rows))
    device = lax.axis_index(("gx", "gy"))
    mixed = local_mix
    for bit in range(count_gy.bit_length() - 1):
        partner = partner_2(mixed, "gy", bit)
        upper_half = lax.axis_index("gy") >> bit & 1 == 1
        mixed = jnp.where(upper_half, partner - mixed, mixed + partner)
    for bit in range(count_gx.bit_length() - 1):
        partner = partner_2(mixed, "gx", bit)
        upper_half = lax.axis_index("gx") >> bit & 1 == 1
        mixed = jnp.where(upper_half, partner - mixed, mixed + partner)
    partial_gram = owner_gram(mixed, samples, local_rows, device)
    gram_total = lax.psum(partial_gram, ("gx", "gy")) / jnp.float32(samples.shape[0])
    factor = jnp.linalg.cholesky(gram_total)
    solved = jax.scipy.linalg.solve_triangular(factor, matrix.T, lower=True)
    return (factor, solved.T)


def solution(mesh):
    in_specs = (P(("gx", "gy"), None), P(("gx", "gy")), P())
    out_specs = (P(), P(("gx", "gy"), None))
    return jax.shard_map(body, mesh=mesh, in_specs=in_specs, out_specs=out_specs, check_vma=False)
```

profile of v0, /device:TPU:1, one launch (start us, length us, event | category | flops | bytes accessed | tf_op | source)
XLA Modules:
  0.0 1037.9 jit_solution(14866249531718413322)
XLA Ops:
  7.2 0.7 convert_element_type.10
  7.9 4.3 convolution_multiply_fusion
  12.2 8.8 collective-permute-start
  21.0 2.3 collective-permute-done
  23.5 1.9 collective-permute-start.1
  25.4 24.3 %collective-permute-done.1 = f32[512,512]{1,0:T(8,128)S(1)} collective-permute-done((f32[512,512]{1,0:T(8,128)S(1)}, f32[512,512]{1,0:T(8,128)S(1)}, u32[]{:S(2)}, u32[]{:S(2)}) %collective-permute-start.1) | collective-permute-done | bytes 1048608 | tf_op jit(solution)/shard_map/ppermute | solution.py:14
  50.0 1.9 collective-permute-start.2
  51.9 24.9 %collective-permute-done.2 = f32[512,512]{1,0:T(8,128)S(1)} collective-permute-done((f32[512,512]{1,0:T(8,128)S(1)}, f32[512,512]{1,0:T(8,128)S(1)}, u32[]{:S(2)}, u32[]{:S(2)}) %collective-permute-start.2) | collective-permute-done | bytes 1048608 | tf_op jit(solution)/shard_map/ppermute | solution.py:14
  77.1 1.9 collective-permute-start.3
  79.0 22.5 %collective-permute-done.3 = f32[512,512]{1,0:T(8,128)S(1)} collective-permute-done((f32[512,512]{1,0:T(8,128)S(1)}, f32[512,512]{1,0:T(8,128)S(1)}, u32[]{:S(2)}, u32[]{:S(2)}) %collective-permute-start.3) | collective-permute-done | bytes 1048608 | tf_op jit(solution)/shard_map/ppermute | solution.py:14
  101.7 1.9 collective-permute-start.4
  103.7 21.6 %collective-permute-done.4 = f32[512,512]{1,0:T(8,128)S(1)} collective-permute-done((f32[512,512]{1,0:T(8,128)S(1)}, f32[512,512]{1,0:T(8,128)S(1)}, u32[]{:S(2)}, u32[]{:S(2)}) %collective-permute-start.4) | collective-permute-done | bytes 1048608 | tf_op jit(solution)/shard_map/ppermute | solution.py:14
  125.5 1.9 collective-permute-start.5
  127.4 48.4 %collective-permute-done.5 = f32[512,512]{1,0:T(8,128)S(1)} collective-permute-done((f32[512,512]{1,0:T(8,128)S(1)}, f32[512,512]{1,0:T(8,128)S(1)}, u32[]{:S(2)}, u32[]{:S(2)}) %collective-permute-start.5) | collective-permute-done | bytes 1048608 | tf_op jit(solution)/shard_map/ppermute | solution.py:14
  176.0 3.4 collective-permute-start.6
  179.5 114.9 %collective-permute-done.6 = f32[512,512]{1,0:T(8,128)S(1)} collective-permute-done((f32[512,512]{1,0:T(8,128)S(1)}, f32[512,512]{1,0:T(8,128)S(1)}, u32[]{:S(2)}, u32[]{:S(2)}) %collective-permute-start.6) | collective-permute-done | bytes 1048608 | tf_op jit(solution)/shard_map/ppermute | solution.py:14
  294.6 10.7 %collective-permute-start.7 = (f32[512,512]{1,0:T(8,128)S(1)}, f32[512,512]{1,0:T(8,128)S(1)}, u32[]{:S(2)}, u32[]{:S(2)}) collective-permute-start(f32[512,512]{1,0:T(8,128)S(1)} %add_select_fusion.1), channel_id=1, source_target_pairs={{0,128},{128,0},{16,144},{144,16},{32,160},{160,32},{48,176},{176,... | collective-permute-start | bytes 3145736 | tf_op jit(solution)/shard_map/ppermute | solution.py:14
  305.4 39.8 %collective-permute-done.7 = f32[512,512]{1,0:T(8,128)S(1)} collective-permute-done((f32[512,512]{1,0:T(8,128)S(1)}, f32[512,512]{1,0:T(8,128)S(1)}, u32[]{:S(2)}, u32[]{:S(2)}) %collective-permute-start.7) | collective-permute-done | bytes 1048608 | tf_op jit(solution)/shard_map/ppermute | solution.py:14
  345.4 55.3 %collective-permute-start.8 = (f32[512,512]{1,0:T(8,128)S(1)}, f32[512,512]{1,0:T(8,128)S(1)}, u32[]{:S(2)}, u32[]{:S(2)}) collective-permute-start(f32[512,512]{1,0:T(8,128)S(1)} %add_select_fusion), channel_id=1, source_target_pairs={{0,256},{256,0},{16,272},{272,16},{32,288},{288,32},{48,304},{304,... | collective-permute-start | bytes 3145736 | tf_op jit(solution)/shard_map/ppermute | solution.py:14
  400.8 1.9 convert_reduce_fusion
  402.7 20.3 %collective-permute-done.8 = f32[512,512]{1,0:T(8,128)S(1)} collective-permute-done((f32[512,512]{1,0:T(8,128)S(1)}, f32[512,512]{1,0:T(8,128)S(1)}, u32[]{:S(2)}, u32[]{:S(2)}) %collective-permute-start.8) | collective-permute-done | bytes 1048608 | tf_op jit(solution)/shard_map/ppermute | solution.py:14
  423.0 3.2 fusion.1
  426.3 463.1 %all-reduce.3.cloned.1.call-done = f32[512,512]{0,1:T(8,128)} async-done(((f32[512,512]{0,1:T(8,128)}), f32[512,512]{0,1:T(8,128)}) %all-reduce.3.cloned.1.call-update) | async-done | bytes 1048592 | tf_op jit(solution)/shard_map/psum | solution.py:59
  889.3 1.3 broadcast_multiply_fusion
  891.0 0.9 copy-done
  892.1 11.7 %cholesky.104 = f32[128,128]{1,0:T(8,128)S(1)} custom-call(f32[128,128]{1,0:T(8,128)S(1)} %cholesky.266), custom_call_target="Cholesky" | custom-call | tf_op jit(solution)/shard_map/jit(cholesky)/cholesky | solution.py:60
  904.0 9.8 custom-call.31
  914.5 11.9 %cholesky.217 = f32[128,128]{1,0:T(8,128)S(1)} custom-call(f32[128,128]{1,0:T(8,128)S(1)} %cholesky.270), custom_call_target="Cholesky" | custom-call | tf_op jit(solution)/shard_map/jit(cholesky)/cholesky | solution.py:60
  926.4 9.8 custom-call.32
  936.9 11.7 %cholesky.238 = f32[128,128]{1,0:T(8,128)S(1)} custom-call(f32[128,128]{1,0:T(8,128)S(1)} %cholesky.275), custom_call_target="Cholesky" | custom-call | tf_op jit(solution)/shard_map/jit(cholesky)/cholesky | solution.py:60
  948.6 0.7 compare_reduce_fusion.1
  949.4 9.8 custom-call.33
  959.8 11.9 %cholesky.255 = f32[128,128]{1,0:T(8,128)S(1)} custom-call(f32[128,128]{1,0:T(8,128)S(1)} %convolution_subtract_fusion.5), custom_call_target="Cholesky" | custom-call | tf_op jit(solution)/shard_map/jit(cholesky)/cholesky | solution.py:60
  971.7 0.6 compare_reduce_fusion
  972.3 0.6 compare_reduce_fusion.2
  975.5 1.2 fusion.43
  976.8 8.5 while.1
  977.5 1.4 bitcast_dynamic-update-slice_fusion.2
  979.0 0.6 fusion.106
  979.6 1.4 bitcast_dynamic-update-slice_fusion.2
  981.1 0.6 fusion.106
  981.7 1.4 bitcast_dynamic-update-slice_fusion.2
  983.2 0.6 fusion.106
  983.8 1.4 bitcast_dynamic-update-slice_fusion.2
  985.3 39.3 %custom-call.34 = f32[4,128,128]{1,2,0:T(8,128)S(1)} custom-call(f32[4,128,128]{2,1,0:T(8,128)S(1)} %get-tuple-element.9), custom_call_target="InvertDiagBlocksLowerTriangular" | custom-call | tf_op jit(solution)/shard_map/jit(_solve_triangular)/triangular_solve | solution.py:61
  1026.1 1.0 convolution_subtract_fusion
  1027.5 1.5 convolution_subtract_fusion.2
  1029.5 1.3 copy.10
  (47 shorter events, 7.9 us)
Async XLA Ops:
  7.2 882.2 %all-reduce.3.cloned.1.call-start = ((), (), s32[]{:S(2)}) async-start(), calls=%async_computation | async-start | bytes 2097152 | tf_op jit(solution)/shard_map/psum | solution.py:59
  12.2 11.1 %collective-permute-start = (f32[512,512]{1,0:T(8,128)S(1)}, f32[512,512]{1,0:T(8,128)S(1)}, u32[]{:S(2)}, u32[]{:S(2)}) collective-permute-start(f32[512,512]{1,0:T(8,128)S(1)} %convolution_multiply_fusion), channel_id=1, source_target_pairs={{0,1},{1,0},{2,3},{3,2},{4,5},{5,4},{6,7},{7,6},{8,9},{9,8},{10,11... | collective-permute-start | bytes 3145736 | tf_op jit(solution)/shard_map/ppermute | solution.py:14
  23.5 26.3 %collective-permute-start.1 = (f32[512,512]{1,0:T(8,128)S(1)}, f32[512,512]{1,0:T(8,128)S(1)}, u32[]{:S(2)}, u32[]{:S(2)}) collective-permute-start(f32[512,512]{1,0:T(8,128)S(1)} %add_select_fusion.7), channel_id=1, source_target_pairs={{0,2},{2,0},{1,3},{3,1},{4,6},{6,4},{5,7},{7,5},{8,10},{10,8},{9,1... | collective-permute-start | bytes 3145736 | tf_op jit(solution)/shard_map/ppermute | solution.py:14
  50.0 26.8 %collective-permute-start.2 = (f32[512,512]{1,0:T(8,128)S(1)}, f32[512,512]{1,0:T(8,128)S(1)}, u32[]{:S(2)}, u32[]{:S(2)}) collective-permute-start(f32[512,512]{1,0:T(8,128)S(1)} %add_select_fusion.6), channel_id=1, source_target_pairs={{0,4},{4,0},{1,5},{5,1},{2,6},{6,2},{3,7},{7,3},{8,12},{12,8},{9,1... | collective-permute-start | bytes 3145736 | tf_op jit(solution)/shard_map/ppermute | solution.py:14
  77.1 24.4 %collective-permute-start.3 = (f32[512,512]{1,0:T(8,128)S(1)}, f32[512,512]{1,0:T(8,128)S(1)}, u32[]{:S(2)}, u32[]{:S(2)}) collective-permute-start(f32[512,512]{1,0:T(8,128)S(1)} %add_select_fusion.5), channel_id=1, source_target_pairs={{0,8},{8,0},{1,9},{9,1},{2,10},{10,2},{3,11},{11,3},{4,12},{12,4},... | collective-permute-start | bytes 3145736 | tf_op jit(solution)/shard_map/ppermute | solution.py:14
  101.7 23.5 %collective-permute-start.4 = (f32[512,512]{1,0:T(8,128)S(1)}, f32[512,512]{1,0:T(8,128)S(1)}, u32[]{:S(2)}, u32[]{:S(2)}) collective-permute-start(f32[512,512]{1,0:T(8,128)S(1)} %add_select_fusion.4), channel_id=1, source_target_pairs={{0,16},{16,0},{32,48},{48,32},{64,80},{80,64},{96,112},{112,96},{1... | collective-permute-start | bytes 3145736 | tf_op jit(solution)/shard_map/ppermute | solution.py:14
  125.5 50.3 %collective-permute-start.5 = (f32[512,512]{1,0:T(8,128)S(1)}, f32[512,512]{1,0:T(8,128)S(1)}, u32[]{:S(2)}, u32[]{:S(2)}) collective-permute-start(f32[512,512]{1,0:T(8,128)S(1)} %add_select_fusion.3), channel_id=1, source_target_pairs={{0,32},{32,0},{16,48},{48,16},{64,96},{96,64},{80,112},{112,80},{1... | collective-permute-start | bytes 3145736 | tf_op jit(solution)/shard_map/ppermute | solution.py:14
  176.0 118.4 %collective-permute-start.6 = (f32[512,512]{1,0:T(8,128)S(1)}, f32[512,512]{1,0:T(8,128)S(1)}, u32[]{:S(2)}, u32[]{:S(2)}) collective-permute-start(f32[512,512]{1,0:T(8,128)S(1)} %add_select_fusion.2), channel_id=1, source_target_pairs={{0,64},{64,0},{16,80},{80,16},{32,96},{96,32},{48,112},{112,48},{1... | collective-permute-start | bytes 3145736 | tf_op jit(solution)/shard_map/ppermute | solution.py:14
  294.6 50.6 %collective-permute-start.7 = (f32[512,512]{1,0:T(8,128)S(1)}, f32[512,512]{1,0:T(8,128)S(1)}, u32[]{:S(2)}, u32[]{:S(2)}) collective-permute-start(f32[512,512]{1,0:T(8,128)S(1)} %add_select_fusion.1), channel_id=1, source_target_pairs={{0,128},{128,0},{16,144},{144,16},{32,160},{160,32},{48,176},{176,... | collective-permute-start | bytes 3145736 | tf_op jit(solution)/shard_map/ppermute | solution.py:14
  305.4 95.4 %copy-start.2 = (s32[2048]{0:T(1024)S(1)}, s32[2048]{0:T(1024)}, u32[]{:S(2)}) copy-start(s32[2048]{0:T(1024)} %param.5) | copy-start | bytes 24580
  345.4 77.6 %collective-permute-start.8 = (f32[512,512]{1,0:T(8,128)S(1)}, f32[512,512]{1,0:T(8,128)S(1)}, u32[]{:S(2)}, u32[]{:S(2)}) collective-permute-start(f32[512,512]{1,0:T(8,128)S(1)} %add_select_fusion), channel_id=1, source_target_pairs={{0,256},{256,0},{16,272},{272,16},{32,288},{288,32},{48,304},{304,... | collective-permute-start | bytes 3145736 | tf_op jit(solution)/shard_map/ppermute | solution.py:14
  890.7 1.2 copy-start
  975.5 49.1 %copy-start.1 = (f32[512,512]{1,0:T(8,128)S(1)}, f32[512,512]{1,0:T(8,128)}, u32[]{:S(2)}) copy-start(f32[512,512]{1,0:T(8,128)} %param.3) | copy-start | bytes 3145732
Sparse Core Ops, SparseCore 0:
  426.4 462.9 all-reduce.2
where the time goes:
time: 1040 us
  waiting for transfers between devices  782 us (75%)
  other arithmetic  125 us (12%)
  starting transfers between devices  87.9 us (8%)
  between operations  17.3 us (2%)
  matrix products  14.1 us (1%)
  local copies, waits for them, and re-layouts  11.1 us (1%)
    psum x1, waiting for transfers between devices, body(): lax.psum(partial_gram, ('gx', 'gy')) / jnp.float32(samples.shape[0])  463 us
    ppermute x9, waiting for transfers between devices, partner_2(): return lax.ppermute(block, axis, route)  319 us
    ppermute x9, starting transfers between devices, partner_2(): return lax.ppermute(block, axis, route)  87.9 us
    another operation x14, other arithmetic, body(): factor = jnp.linalg.cholesky(gram_total)  78.8 us
    another operation x3, other arithmetic, body(): solved = jax.scipy.linalg.solve_triangular(factor, matrix.T, lower=True)  40.6 us
  transfers between devices with their start and end apart: 10, of which 10 were waited for; matrix products, arithmetic and copies ran while one was open for 0% of the time, Pallas kernels for 0%

commit v1 on v0

v1 whole, which is shorter than its diff:
```python
import jax
import jax.numpy as jnp
from jax import lax
from jax.experimental import pallas as pl
from jax.experimental.pallas import tpu as pltpu
from jax.sharding import Mesh
from jax.sharding import PartitionSpec as P

BLOCK = 128
PANEL = 8
CHUNK = 256
ROW_AXES = ("x_hi", "z", "x_lo", "y", "core")
PLANE = ("x_hi", "x_lo", "y", "core")
NN = ((1,), (0,))
NT = ((1,), (1,))


def split2(x):
    hi = x.astype(jnp.bfloat16)
    lo = (x - hi.astype(jnp.float32)).astype(jnp.bfloat16)
    return hi, lo


def dot3(a, b, dims):
    (ah, al), (bh, bl) = a, b
    dg = lambda p, q: lax.dot_general(p, q, (dims, ((), ())), preferred_element_type=jnp.float32)
    return dg(ah, bh) + (dg(ah, bl) + dg(al, bh))


def factor_block(rows):
    count = len(rows)
    lane = lax.broadcasted_iota(jnp.int32, (PANEL, BLOCK), 1)
    sub = lax.broadcasted_iota(jnp.int32, (PANEL, BLOCK), 0)
    rows = list(rows)
    upper, inverse = [], []
    full = (PANEL, BLOCK)
    for k in range(count):
        base = k * PANEL
        own = (lane >= base) & (lane < base + PANEL)
        panel = rows[k]
        piv = {}
        for j in range(PANEL):
            col = jnp.broadcast_to(panel[:, base + j : base + j + 1], full)
            for i in range(j, PANEL):
                piv[i, j] = jnp.broadcast_to(col[i : i + 1, :], full)
        cols = {}
        for r in range(k + 1, count):
            for j in range(PANEL):
                cols[r, j] = jnp.broadcast_to(rows[r][:, base + j : base + j + 1], full)
        root, inv, low = [], [], {}
        for j in range(PANEL):
            s = lax.rsqrt(piv[j, j])
            root.append(s)
            d = s * s
            inv.append(d)
            for i in range(j + 1, PANEL):
                low[i, j] = piv[i, j] * d
            for i in range(j + 1, PANEL):
                for m in range(j + 1, i + 1):
                    piv[i, m] = piv[i, m] - low[i, j] * piv[m, j]
        masked = jnp.where(own, jnp.where(lane - base == sub, 1.0, 0.0), panel)
        fwd_u, fwd_w = [], []
        for i in range(PANEL):
            u = jnp.broadcast_to(panel[i : i + 1, :], full)
            w = jnp.broadcast_to(masked[i : i + 1, :], full)
            for j in range(i):
                u = u - low[i, j] * fwd_u[j]
                w = w - low[i, j] * fwd_w[j]
            fwd_u.append(u)
            fwd_w.append(w)
        back = [None] * PANEL
        for i in reversed(range(PANEL)):
            v = fwd_w[i] * inv[i]
            for j in range(i + 1, PANEL):
                v = v - low[j, i] * back[j]
            back[i] = v
        for r in range(k + 1, count):
            acc = cols[r, 0] * back[0]
            for j in range(1, PANEL):
                acc = acc + cols[r, j] * back[j]
            rows[r] = jnp.where(own, 0.0, rows[r]) - acc
        up, wp = fwd_u[0] * root[0], fwd_w[0] * root[0]
        for i in range(1, PANEL):
            up = jnp.where(sub == i, fwd_u[i] * root[i], up)
            wp = jnp.where(sub == i, fwd_w[i] * root[i], wp)
        upper.append(jnp.where(lane - base >= sub, up, 0.0))
        inverse.append(jnp.where(lane - base <= sub, wp, 0.0))
    return upper, inverse


def chol_kernel(g_ref, x_ref, l_ref, o_ref, a_ref, w_ref):
    n = g_ref.shape[0]
    a_ref[...] = g_ref[...]
    nb = n // BLOCK
    xs = split2(x_ref[...])
    for kb in range(nb):
        lo, hi = kb * BLOCK, (kb + 1) * BLOCK
        panels = [a_ref[lo + p * PANEL : lo + (p + 1) * PANEL, lo:hi] for p in range(BLOCK // PANEL)]
        upper, inverse = factor_block(panels)
        u = jnp.concatenate(upper, axis=0)
        w = jnp.concatenate(inverse, axis=0)
        l_ref[lo:hi, lo:hi] = u.T
        w_ref[lo:hi, lo:hi] = w
        ws = split2(w)
        if hi < n:
            l_ref[lo:hi, hi:] = jnp.zeros((BLOCK, n - hi), jnp.float32)
            below = dot3(split2(a_ref[hi:, lo:hi]), ws, NT)
            l_ref[hi:, lo:hi] = below
            bs = split2(below)
            a_ref[hi:, hi:] = a_ref[hi:, hi:] - dot3(bs, bs, NT)
        if kb:
            t = dot3(split2(l_ref[lo:hi, :lo]), split2(w_ref[:lo, :lo]), NN)
            w_ref[lo:hi, :lo] = -dot3(ws, split2(t), NN)
        if hi < n:
            w_ref[lo:hi, hi:] = jnp.zeros((BLOCK, n - hi), jnp.float32)
        wrow = split2(w_ref[lo:hi, :hi])
        xk = (xs[0][:, :hi], xs[1][:, :hi])
        o_ref[:, lo:hi] = dot3(xk, wrow, NT)


def chol_solve(gram, x):
    n = gram.shape[0]
    shape = jax.ShapeDtypeStruct((n, n), jnp.float32)
    return pl.pallas_call(
        chol_kernel,
        out_shape=(shape, jax.ShapeDtypeStruct(x.shape, jnp.float32)),
        in_specs=[pl.BlockSpec(memory_space=pltpu.VMEM)] * 2,
        out_specs=[pl.BlockSpec(memory_space=pltpu.VMEM)] * 2,
        scratch_shapes=[pltpu.VMEM((n, n), jnp.float32)] * 2,
        compiler_params=pltpu.CompilerParams(vmem_limit_bytes=32 * 1024 * 1024),
    )(gram, x)


def signs_of(value, count):
    v = lax.broadcasted_iota(jnp.int32, (count, value.shape[1]), 0) & value
    for shift in (4, 2, 1):
        v = v ^ (v >> shift)
    return (1 - 2 * (v & 1)).astype(jnp.float32)


def mix_kernel(pos_ref, x_ref, samples_ref, o_ref, h_ref):
    width = x_ref.shape[0]
    depth = x_ref.shape[1]
    sources = 32
    cols = width // sources
    hi, lo = split2(x_ref[...])
    z_bits = pos_ref[0]
    scale = 1.0 / 512.0
    for c in range(samples_ref.shape[1] // CHUNK):
        s = samples_ref[:, c * CHUNK : (c + 1) * CHUNK]
        within = s & (depth - 1)
        device = s // depth
        low = signs_of(within & 15, 16)
        high = signs_of(within // 16, depth // 16)
        for r in range(depth // 16):
            h_ref[r * 16 : (r + 1) * 16, :] = (low * high[r : r + 1, :]).astype(jnp.bfloat16)
        plane_sign = signs_of((device & 15) | ((device // 256) * 16), sources)
        zv = (device // 16) & z_bits
        zv = zv ^ (zv >> 2)
        zv = zv ^ (zv >> 1)
        z_sign = (1 - 2 * (zv & 1)).astype(jnp.float32) * scale
        h = h_ref[...]
        t = jnp.dot(hi, h, preferred_element_type=jnp.float32)
        t = t + jnp.dot(lo, h, preferred_element_type=jnp.float32)
        acc = t[:cols, :]
        for p in range(1, sources):
            acc = acc + t[p * cols : (p + 1) * cols, :] * plane_sign[p : p + 1, :]
        acc = acc * z_sign
        for b in range(CHUNK // BLOCK):
            o_ref[c * (CHUNK // BLOCK) + b] = acc[:, b * BLOCK : (b + 1) * BLOCK]


def sample_columns(columns, samples, z_index):
    width = columns.shape[0]
    count = samples.shape[0]
    return pl.pallas_call(
        mix_kernel,
        out_shape=jax.ShapeDtypeStruct((count // BLOCK, width // 32, BLOCK), jnp.float32),
        in_specs=[
            pl.BlockSpec(memory_space=pltpu.SMEM),
            pl.BlockSpec(memory_space=pltpu.VMEM),
            pl.BlockSpec(memory_space=pltpu.VMEM),
        ],
        out_specs=pl.BlockSpec(memory_space=pltpu.VMEM),
        scratch_shapes=[pltpu.VMEM((columns.shape[1], CHUNK), jnp.bfloat16)],
        compiler_params=pltpu.CompilerParams(vmem_limit_bytes=32 * 1024 * 1024),
    )(z_index.reshape(1), columns, samples.reshape(1, count))


def exchange(block, axes):
    return lax.all_to_all(block, axes, 0, 0, tiled=True)


def gather(block, axes):
    count = lax.axis_size(axes)
    return exchange(jnp.broadcast_to(block[None], (count,) + block.shape), axes)


def body(matrix, signs, samples):
    n = matrix.shape[1]
    plane = lax.axis_size(PLANE)
    depth = lax.axis_size("z")
    cols = n // plane
    z_index = lax.axis_index("z")
    signed = (signs.astype(jnp.float32)[:, None] * matrix).T
    columns = exchange(signed.reshape(plane, cols, -1), PLANE)
    partial = sample_columns(columns.reshape(n, -1), samples, z_index)
    mine = jnp.sum(exchange(partial, "z"), axis=0)
    every = gather(mine, PLANE).reshape(n, -1)
    rows = lax.dot_general(mine, every, (NT, ((), ())), precision=lax.Precision.HIGHEST)
    rows = rows.reshape(depth, cols // depth, n)
    row = jnp.sum(exchange(rows, "z"), axis=0) / jnp.float32(samples.shape[0])
    rows = gather(row, "z").reshape(cols, n)
    gram = gather(rows, PLANE).reshape(n, n)
    return chol_solve(gram, matrix)


def solution(mesh):
    fine = Mesh(mesh.devices.reshape(2, 16, 2, 4, 2), ROW_AXES)
    in_specs = (P(ROW_AXES, None), P(ROW_AXES), P())
    out_specs = (P(), P(ROW_AXES, None))
    return jax.shard_map(body, mesh=fine, in_specs=in_specs, out_specs=out_specs, check_vma=False)
```

time: 1040 us -> 155 us (0.15)
  waiting for transfers between devices: 782 us -> 17 us
  other arithmetic: 125 us -> 1.85 us
  blocking collectives: 0 us -> 92.6 us
  starting transfers between devices: 87.9 us -> 10.5 us
  Pallas kernels: 0 us -> 29.4 us
  between operations: 17.3 us -> 0.71 us
  matrix products: 14.1 us -> 0.31 us
    psum x1 -> x0, waiting for transfers between devices: 463 us -> none  [body(): lax.psum(partial_gram, ('gx', 'gy')) / jnp.float32(samples.shape[0])]
    ppermute x9 -> x0, waiting for transfers between devices: 319 us -> none  [partner_2(): return lax.ppermute(block, axis, route)]
    another operation x17 -> x0, other arithmetic: 119 us -> none  [the longest x14 78.8 us: body(): factor = jnp.linalg.cholesky(gram_total)]
    all_to_all x0 -> x5, blocking collectives: none -> 92.6 us  [exchange(): return lax.all_to_all(block, axes, 0, 0, tiled=True)]
    ppermute x9 -> x0, starting transfers between devices: 87.9 us -> none  [partner_2(): return lax.ppermute(block, axis, route)]
    pallas_call x0 -> x2, Pallas kernels: none -> 29.4 us  [the longest x1 27 us: chol_solve(): pl.pallas_call(chol_kernel, out_shape=(shape, jax.ShapeDtypeStruct(x.shap...]
    all_to_all x0 -> x1, waiting for transfers between devices: none -> 17 us  [exchange(): return lax.all_to_all(block, axes, 0, 0, tiled=True)]
    all_to_all x0 -> x1, starting transfers between devices: none -> 10.5 us  [exchange(): return lax.all_to_all(block, axes, 0, 0, tiled=True)]
  transfers between devices with their start and end apart: 10 -> 1, of which waited for: 10 -> 1; matrix products, arithmetic and copies ran while one was open for 0% -> 0% of each run, Pallas kernels for 0% -> 0%
where the time goes in v1:
time: 155 us; the launch traced here: 154 us
  blocking collectives  92.6 us (60%)
  Pallas kernels  29.4 us (19%)
  waiting for transfers between devices  17 us (11%)
  starting transfers between devices  10.5 us (7%)
  other arithmetic  1.85 us (1%)
  local copies, waits for them, and re-layouts  1.77 us (1%)
    all_to_all x5, blocking collectives, exchange(): return lax.all_to_all(block, axes, 0, 0, tiled=True)  92.6 us
    pallas_call x1, Pallas kernels, chol_solve(): pl.pallas_call(chol_kernel, out_shape=(shape, jax.ShapeDtypeStruct(x.shap...  27 us
    all_to_all x1, waiting for transfers between devices, exchange(): return lax.all_to_all(block, axes, 0, 0, tiled=True)  17 us
    all_to_all x1, starting transfers between devices, exchange(): return lax.all_to_all(block, axes, 0, 0, tiled=True)  10.5 us
  transfers between devices with their start and end apart: 1, of which 1 were waited for; matrix products, arithmetic and copies ran while one was open for 0% of the time, Pallas kernels for 0%

profile of v1, /device:TPU:1, one launch (start us, length us, event | category | flops | bytes accessed | tf_op | source)
XLA Modules:
  0.0 154.1 jit_solution(8526807631494737130)
XLA Ops:
  0.6 0.7 convert_element_type.3
  1.3 1.6 %copy.7 = f32[512,512]{0,1:T(8,128)S(1)} copy(f32[512,512]{1,0:T(8,128)} %x_ref.1) | data formatting | bytes 2097152 | tf_op args[0]
  2.9 1.1 broadcast_multiply_fusion
  4.0 10.5 %all-to-all-start = ((f32[32,16,512]{2,1,0:T(8,128)}), f32[32,16,512]{2,1,0:T(8,128)S(1)}, u32[]{:S(2)}, u32[]{:S(2)}) async-start(f32[32,16,512]{2,1,0:T(8,128)} %bitcast.2), calls=%async_computation | async-start | bytes 2097152 | tf_op jit(solution)/shard_map/all_to_all | solution.py:191
  14.4 0.0 copy-start.1
  14.5 17.0 %all-to-all-done = f32[32,16,512]{2,1,0:T(8,128)S(1)} async-done(((f32[32,16,512]{2,1,0:T(8,128)}), f32[32,16,512]{2,1,0:T(8,128)S(1)}, u32[]{:S(2)}, u32[]{:S(2)}) %all-to-all-start) | async-done | bytes 1048608 | tf_op jit(solution)/shard_map/all_to_all | solution.py:191
  31.4 0.0 copy-done.1
  31.4 2.4 %shard_map.50 = f32[16,16,128]{2,1,0:T(8,128)S(1)} custom-call(s32[1]{0:T(128)} %bitcast.pos_ref, f32[512,512]{1,0:T(8,128)S(1)} %bitcast.15, s32[1,2048]{1,0:T(1,128)S(1)} %bitcast.17), custom_call_target="tpu_custom_call" | custom-call | tf_op jit(solution)/shard_map/pallas_call | solution.py:176
  33.9 24.9 %all_to_all.30 = f32[16,16,128]{2,1,0:T(8,128)S(1)} all-to-all(f32[16,16,128]{2,1,0:T(8,128)S(1)} %shard_map.50), channel_id=1, replica_groups=mesh['x_hi'=2,'z'=16,'x_lo'=2,'y'=4,'core'=2] {'z'}, dimensions={0} | all-to-all | bytes 262144 | tf_op jit(solution)/shard_map/all_to_all | solution.py:191
  58.8 15.7 %all_to_all.31 = f32[32,16,128]{2,1,0:T(8,128)S(1)} all-to-all(f32[32,16,128]{2,1,0:T(8,128)S(1)} %broadcast_in_dim.8), channel_id=1, replica_groups=mesh['x_hi'=2,'z'=16,'x_lo'=2,'y'=4,'core'=2] {'x_hi','x_lo','y','core'}, dimensions={0} | all-to-all | bytes 524288 | tf_op jit(solution)/shard_map/all_to_all | solution.py:191
  74.5 0.3 convolution_bitcast_fusion
  74.9 15.0 %all_to_all.32 = f32[16,1,512]{2,1,0:T(1,128)S(1)} all-to-all(f32[16,1,512]{2,1,0:T(1,128)S(1)} %copy.8), channel_id=1, replica_groups=mesh['x_hi'=2,'z'=16,'x_lo'=2,'y'=4,'core'=2] {'z'}, dimensions={0} | all-to-all | bytes 65536 | tf_op jit(solution)/shard_map/all_to_all | solution.py:191
  89.9 14.0 %all_to_all.33 = f32[16,1,512]{2,1,0:T(1,128)S(1)} all-to-all(f32[16,1,512]{2,1,0:T(1,128)S(1)} %broadcast_in_dim.9), channel_id=1, replica_groups=mesh['x_hi'=2,'z'=16,'x_lo'=2,'y'=4,'core'=2] {'z'}, dimensions={0} | all-to-all | bytes 65536 | tf_op jit(solution)/shard_map/all_to_all | solution.py:191
  103.9 0.1 broadcast_in_dim.11
  104.0 0.0 copy-start
  104.1 23.1 %all_to_all.34 = f32[32,16,512]{2,1,0:T(8,128)S(1)} all-to-all(f32[32,16,512]{2,1,0:T(8,128)S(1)} %broadcast_in_dim.11), channel_id=1, replica_groups=mesh['x_hi'=2,'z'=16,'x_lo'=2,'y'=4,'core'=2] {'x_hi','x_lo','y','core'}, dimensions={0} | all-to-all | bytes 2097152 | tf_op jit(solution)/shard_map/all_to_all | solution.py:191
  127.2 0.0 copy-done
  127.2 27.0 %shard_map.51 = (f32[512,512]{1,0:T(8,128)}, f32[512,512]{1,0:T(8,128)}) custom-call(f32[512,512]{1,0:T(8,128)S(1)} %bitcast.16, f32[512,512]{1,0:T(8,128)S(1)} %copy-done), custom_call_target="tpu_custom_call" | custom-call | tf_op jit(solution)/shard_map/pallas_call | solution.py:124
  (7 shorter events, 0.2 us)
Async XLA Ops:
  4.0 27.5 %all-to-all-start = ((f32[32,16,512]{2,1,0:T(8,128)}), f32[32,16,512]{2,1,0:T(8,128)S(1)}, u32[]{:S(2)}, u32[]{:S(2)}) async-start(f32[32,16,512]{2,1,0:T(8,128)} %bitcast.2), calls=%async_computation | async-start | bytes 2097152 | tf_op jit(solution)/shard_map/all_to_all | solution.py:191
  14.4 17.0 %copy-start.1 = (s32[2048]{0:T(1024)S(1)}, s32[2048]{0:T(1024)}, u32[]{:S(2)}) copy-start(s32[2048]{0:T(1024)} %param.5) | copy-start | bytes 24580
  104.0 23.1 %copy-start = (f32[512,512]{1,0:T(8,128)S(1)}, f32[512,512]{1,0:T(8,128)}, u32[]{:S(2)}) copy-start(f32[512,512]{1,0:T(8,128)} %x_ref.1) | copy-start | bytes 3145732

commit v2 on v0

v2 whole, which is shorter than its diff:
```python
import jax
import jax.numpy as jnp
from jax import lax
from jax.experimental import pallas as pl
from jax.experimental.pallas import tpu as pltpu
from jax.sharding import Mesh
from jax.sharding import PartitionSpec as P

BLOCK = 128
CHUNK = 512
ROW_AXES = ("x_hi", "z_hi", "z_lo", "x_lo", "y", "core")
PLANE = ("x_hi", "x_lo", "y", "core")
LOWER = ((0, 0), (1, 0), (1, 1), (2, 0), (2, 1), (2, 2), (3, 0), (3, 1), (3, 2), (3, 3))
VMEM = pl.BlockSpec(memory_space=pltpu.VMEM)
SMEM = pl.BlockSpec(memory_space=pltpu.SMEM)
PARAMS = pltpu.CompilerParams(vmem_limit_bytes=32 * 1024 * 1024)


def split2(x):
    hi = x.astype(jnp.bfloat16)
    return hi, (x - hi.astype(jnp.float32)).astype(jnp.bfloat16)


def left(x):
    hi, lo = split2(x)
    return jnp.concatenate([hi, hi, lo], axis=1)


def right(x):
    hi, lo = split2(x)
    return jnp.concatenate([hi, lo, hi], axis=1)


def dot_t(a, b):
    return lax.dot_general(a, b, (((1,), (1,)), ((), ())), preferred_element_type=jnp.float32)


def factor_block(rows, c_ref):
    lane = lax.broadcasted_iota(jnp.int32, (8, BLOCK), 1)
    sub = lax.broadcasted_iota(jnp.int32, (8, BLOCK), 0)
    rows = list(rows)
    groups = len(rows)
    full = (8, BLOCK)
    upper, packed = [], []
    for k in range(groups):
        base = k * 8
        own = (lane >= base) & (lane < base + 8)
        panel = rows[k]
        col = [jnp.broadcast_to(panel[:, base + j : base + j + 1], full) for j in range(8)]
        for j in range(8):
            c_ref[k % 2, j] = col[j]
        c_ref[k % 2, 8] = panel
        spread = lambda j, i: jnp.broadcast_to(c_ref[k % 2, j, i : i + 1, :], full)
        piv = {(i, j): spread(j, i) for i in range(8) for j in range(i + 1)}
        root, inv, low, ratio = {}, {}, {}, {}
        for j in range(0, 8, 2):
            x, y, z = piv[j, j], piv[j + 1, j], piv[j + 1, j + 1]
            det = x * z - y * y
            rest = range(j + 2, 8)
            num = {}
            for i in rest:
                p, q = piv[i, j], piv[i, j + 1]
                num[i] = (p * z - q * y, q * x - p * y)
            rd = 1.0 / det
            for i in rest:
                low[i, j], low[i, j + 1] = num[i][0] * rd, num[i][1] * rd
                for m in range(j + 2, i + 1):
                    piv[i, m] = piv[i, m] - (num[i][0] * piv[m, j] + num[i][1] * piv[m, j + 1]) * rd
            inv[j] = (z * rd, y * rd, x * rd)
            root[j] = lax.rsqrt(x)
            root[j + 1] = lax.rsqrt(det) * (x * root[j])
            ratio[j] = y * (root[j] * root[j])
        fwd = []
        for i in range(8):
            w = jnp.where(own, jnp.where(lane == base + i, 1.0, 0.0), spread(8, i))
            for j in range(i - i % 2):
                w = w - low[i, j] * fwd[j]
            fwd.append(w)
        back = [None] * 8
        for i in reversed(range(0, 8, 2)):
            f, g = fwd[i], fwd[i + 1]
            x, y, z = inv[i]
            v, w = f * x - g * y, g * z - f * y
            for j in range(i + 2, 8):
                v = v - low[j, i] * back[j]
                w = w - low[j, i + 1] * back[j]
            back[i], back[i + 1] = v, w
        for r in range(k + 1, groups):
            terms = [jnp.broadcast_to(rows[r][:, base + j : base + j + 1], full) * back[j] for j in range(8)]
            while len(terms) > 1:
                terms = [x + y for x, y in zip(terms[::2], terms[1::2])]
            rows[r] = jnp.where(own, 0.0, rows[r]) - terms[0]
        up = pk = jnp.zeros(full, jnp.float32)
        for g in range(8):
            h = g - g % 2
            w = (fwd[g] if g == h else fwd[g] - ratio[h] * fwd[h]) * root[g]
            u = w
            for j in range(g, 8):
                e = piv[j, g] if g == h else piv[j, g] - ratio[h] * piv[j, h]
                u = jnp.where(lane == base + j, e * root[g], u)
            up = jnp.where(sub == g, u, up)
            pk = jnp.where(sub == g, w, pk)
        upper.append(jnp.where(lane >= base + sub, up, 0.0))
        packed.append(pk)
    inverse = [jnp.where(lane <= k * 8 + sub, packed[k], 0.0) for k in range(groups)]
    return upper, inverse


def chol_kernel(g_ref, x_ref, l_ref, o_ref, a_ref, c_ref):
    n = x_ref.shape[1]
    nb = n // BLOCK
    at = [slice(k * BLOCK, (k + 1) * BLOCK) for k in range(nb)]
    r = lax.broadcasted_iota(jnp.int32, (BLOCK, BLOCK), 0)
    c = lax.broadcasted_iota(jnp.int32, (BLOCK, BLOCK), 1)
    row_scale, col_scale, row_root = [], [], []
    for k in range(nb):
        for i in range(k, nb):
            a_ref[at[i], at[k]] = lower_block(g_ref, i, k)
        diag = jnp.where(r == c, a_ref[at[k], at[k]], 0.0)
        by_row = jnp.broadcast_to(jnp.sum(diag, axis=1, keepdims=True), (BLOCK, BLOCK))
        s = lax.rsqrt(by_row)
        row_scale.append(s)
        row_root.append(by_row * s)
        col_scale.append(lax.rsqrt(jnp.sum(diag, axis=0, keepdims=True)))
    for k in range(nb):
        for i in range(k, nb):
            a_ref[at[i], at[k]] = a_ref[at[i], at[k]] * row_scale[i] * col_scale[k]
        o_ref[:, at[k]] = x_ref[:, at[k]] * col_scale[k]
    for k in range(nb):
        panels = [a_ref[k * BLOCK + p * 8 : k * BLOCK + (p + 1) * 8, at[k]] for p in range(BLOCK // 8)]
        upper, inverse = factor_block(panels, c_ref)
        ws = right(jnp.concatenate(inverse, axis=0))
        below = {}
        for i in range(k + 1, nb):
            below[i] = dot_t(left(a_ref[at[i], at[k]]), ws)
            for j in range(k + 1, i + 1):
                a_ref[at[i], at[j]] = a_ref[at[i], at[j]] - dot_t(left(below[i]), right(below[j]))
        l_ref[at[k], at[k]] = jnp.concatenate(upper, axis=0).T * row_root[k]
        solved = dot_t(left(o_ref[:, at[k]]), ws)
        o_ref[:, at[k]] = solved
        for i in range(k + 1, nb):
            l_ref[at[i], at[k]] = below[i] * row_root[i]
            l_ref[at[k], at[i]] = jnp.zeros((BLOCK, BLOCK), jnp.float32)
            o_ref[:, at[i]] = o_ref[:, at[i]] - dot_t(left(solved), right(below[i]))


def lower_block(g_ref, i, j):
    core, slot = divmod(LOWER.index((i, j)), len(LOWER) // 2)
    parts = [g_ref[chip * 2 + core, slot * 8 : slot * 8 + 8, :] for chip in range(BLOCK // 8)]
    return jnp.concatenate(parts, axis=0)


def chol_solve(parts, x):
    n = x.shape[1]
    return pl.pallas_call(
        chol_kernel,
        out_shape=(jax.ShapeDtypeStruct((n, n), jnp.float32), jax.ShapeDtypeStruct(x.shape, jnp.float32)),
        in_specs=[VMEM, VMEM],
        out_specs=[VMEM, VMEM],
        scratch_shapes=[pltpu.VMEM((n, n), jnp.float32), pltpu.VMEM((2, 9, 8, BLOCK), jnp.float32)],
        compiler_params=PARAMS,
    )(parts, x)


def gram_kernel(place_ref, p_ref, o_ref, split_ref):
    chip, core = place_ref[0], place_ref[1]
    half = len(LOWER) // 2
    split_ref[...] = right(p_ref[...])
    for slot in range(half):
        i = jnp.where(core == 0, LOWER[slot][0], LOWER[slot + half][0])
        j = jnp.where(core == 0, LOWER[slot][1], LOWER[slot + half][1])
        rows = p_ref[pl.ds(pl.multiple_of(i * BLOCK + chip * 8, 8), 8), :]
        cols = split_ref[pl.ds(pl.multiple_of(j * BLOCK, BLOCK), BLOCK), :]
        o_ref[slot * 8 : slot * 8 + 8, :] = dot_t(left(rows), cols)


def gram_part(columns, place):
    n, depth = columns.shape
    return pl.pallas_call(
        gram_kernel,
        out_shape=jax.ShapeDtypeStruct((4 * len(LOWER), BLOCK), jnp.float32),
        in_specs=[SMEM, VMEM],
        out_specs=VMEM,
        scratch_shapes=[pltpu.VMEM((n, 3 * depth), jnp.bfloat16)],
        compiler_params=PARAMS,
    )(place, columns)


def flip_kernel(x_ref, signs_ref, o_ref):
    o_ref[...] = x_ref[...].T * signs_ref[...].astype(jnp.float32)


def signed_columns(matrix, signs):
    return pl.pallas_call(
        flip_kernel,
        out_shape=jax.ShapeDtypeStruct(matrix.shape[::-1], jnp.float32),
        in_specs=[VMEM, VMEM],
        out_specs=VMEM,
        compiler_params=PARAMS,
    )(matrix, signs.reshape(1, -1))


def signs_of(value, count):
    v = lax.broadcasted_iota(jnp.int32, (count, value.shape[1]), 0) & value
    for shift in (4, 2, 1):
        v = v ^ (v >> shift)
    return (1 - 2 * (v & 1)).astype(jnp.float32)


def mix_kernel(pos_ref, x_ref, samples_ref, o_ref, h_ref):
    width = x_ref.shape[0]
    depth = x_ref.shape[1]
    sources = 32
    cols = width // sources
    hi, lo = split2(x_ref[...])
    z_bits = pos_ref[0]
    scale = 1.0 / 512.0
    for c in range(samples_ref.shape[1] // CHUNK):
        s = samples_ref[:, c * CHUNK : (c + 1) * CHUNK]
        within = s & (depth - 1)
        device = s // depth
        low = signs_of(within & 15, 16)
        high = signs_of(within // 16, depth // 16)
        for r in range(depth // 16):
            h_ref[r * 16 : (r + 1) * 16, :] = (low * high[r : r + 1, :]).astype(jnp.bfloat16)
        plane_sign = signs_of((device & 15) | ((device // 256) * 16), sources)
        zv = (device // 16) & z_bits
        zv = zv ^ (zv >> 2)
        zv = zv ^ (zv >> 1)
        z_sign = (1 - 2 * (zv & 1)).astype(jnp.float32) * scale
        h = h_ref[...]
        t = jnp.dot(hi, h, preferred_element_type=jnp.float32)
        t = t + jnp.dot(lo, h, preferred_element_type=jnp.float32)
        acc = t[:cols, :]
        for p in range(1, sources):
            acc = acc + t[p * cols : (p + 1) * cols, :] * plane_sign[p : p + 1, :]
        acc = acc * z_sign
        o_ref[c] = acc


def sample_columns(columns, samples, z_index):
    width = columns.shape[0]
    count = samples.shape[0]
    return pl.pallas_call(
        mix_kernel,
        out_shape=jax.ShapeDtypeStruct((count // CHUNK, width // 32, CHUNK), jnp.float32),
        in_specs=[SMEM, VMEM, VMEM],
        out_specs=VMEM,
        scratch_shapes=[pltpu.VMEM((columns.shape[1], CHUNK), jnp.bfloat16)],
        compiler_params=PARAMS,
    )(z_index.reshape(1), columns, samples.reshape(1, count))


def exchange(block, axes):
    return lax.all_to_all(block, axes, 0, 0, tiled=True)


def gather(block, axes):
    count = lax.axis_size(axes)
    return exchange(jnp.broadcast_to(block[None], (count,) + block.shape), axes)


def body(matrix, signs, samples):
    rows, n = matrix.shape
    plane = lax.axis_size(PLANE)
    place = lax.axis_index(PLANE)
    columns = exchange(signed_columns(matrix, signs).reshape(plane, n // plane, rows), PLANE)
    partial = sample_columns(columns.reshape(n, rows), samples, lax.axis_index(("z_hi", "z_lo")))
    mine = jnp.sum(exchange(partial, "z_lo"), axis=0)
    mine = jnp.sum(gather(mine, "z_hi"), axis=0)
    every = gather(mine, PLANE).reshape(n, -1)
    part = gram_part(every, jnp.stack([place // 2, place % 2]))
    part = jnp.sum(gather(part, "z_lo"), axis=0) / jnp.float32(samples.shape[0])
    return chol_solve(gather(part, PLANE), matrix)


def solution(mesh):
    fine = Mesh(mesh.devices.reshape(2, 4, 4, 2, 4, 2), ROW_AXES)
    in_specs = (P(ROW_AXES, None), P(ROW_AXES), P())
    out_specs = (P(), P(ROW_AXES, None))
    return jax.shard_map(body, mesh=fine, in_specs=in_specs, out_specs=out_specs, check_vma=False)
```

time: 1040 us -> 134 us (0.13)
  waiting for transfers between devices: 782 us -> 33.9 us
  other arithmetic: 125 us -> 0.11 us
  starting transfers between devices: 87.9 us -> 18.5 us
  blocking collectives: 0 us -> 57.7 us
  Pallas kernels: 0 us -> 19.3 us
  between operations: 17.3 us -> 0.75 us
  matrix products: 14.1 us -> 0 us
    psum x1 -> x0, waiting for transfers between devices: 463 us -> none  [body(): lax.psum(partial_gram, ('gx', 'gy')) / jnp.float32(samples.shape[0])]
    ppermute x9 -> x0, waiting for transfers between devices: 319 us -> none  [partner_2(): return lax.ppermute(block, axis, route)]
    another operation x17 -> x1, other arithmetic: 119 us -> 0.08 us  [body(): part = gram_part(every, jnp.stack([place // 2, place % 2]))]
    ppermute x9 -> x0, starting transfers between devices: 87.9 us -> none  [partner_2(): return lax.ppermute(block, axis, route)]
    all_to_all x0 -> x4, blocking collectives: none -> 57.7 us  [exchange(): return lax.all_to_all(block, axes, 0, 0, tiled=True)]
    all_to_all x0 -> x2, waiting for transfers between devices: none -> 33.9 us  [exchange(): return lax.all_to_all(block, axes, 0, 0, tiled=True)]
    pallas_call x0 -> x4, Pallas kernels: none -> 19.3 us  [the longest x1 14.3 us: chol_solve(): pl.pallas_call(chol_kernel, out_shape=(jax.ShapeDtypeStruct((n, n), jnp.f...]
    all_to_all x0 -> x2, starting transfers between devices: none -> 18.5 us  [exchange(): return lax.all_to_all(block, axes, 0, 0, tiled=True)]
  transfers between devices with their start and end apart: 10 -> 2, of which waited for: 10 -> 2; matrix products, arithmetic and copies ran while one was open for 0% -> 0% of each run, Pallas kernels for 0% -> 0%
where the time goes in v2:
time: 134 us; the launch traced here: 133 us
  blocking collectives  57.7 us (43%)
  waiting for transfers between devices  33.9 us (25%)
  Pallas kernels  19.3 us (14%)
  starting transfers between devices  18.5 us (14%)
  local copies, waits for them, and re-layouts  3.09 us (2%)
    all_to_all x4, blocking collectives, exchange(): return lax.all_to_all(block, axes, 0, 0, tiled=True)  57.7 us
    all_to_all x2, waiting for transfers between devices, exchange(): return lax.all_to_all(block, axes, 0, 0, tiled=True)  33.9 us
    all_to_all x2, starting transfers between devices, exchange(): return lax.all_to_all(block, axes, 0, 0, tiled=True)  18.5 us
    pallas_call x1, Pallas kernels, chol_solve(): pl.pallas_call(chol_kernel, out_shape=(jax.ShapeDtypeStruct((n, n), jnp.f...  14.3 us
  transfers between devices with their start and end apart: 2, of which 2 were waited for; matrix products, arithmetic and copies ran while one was open for 0% of the time, Pallas kernels for 0%

profile of v2, /device:TPU:1, one launch (start us, length us, event | category | flops | bytes accessed | tf_op | source)
XLA Modules:
  0.0 133.3 jit_solution(6998165147908268672)
XLA Ops:
  0.6 0.0 copy-start
  0.6 1.2 copy-done
  1.9 0.0 copy-start.3
  1.9 0.7 copy-done.3
  2.5 1.3 shard_map.50
  3.8 10.5 %all-to-all-start = ((f32[32,16,512]{2,1,0:T(8,128)}), f32[32,16,512]{2,1,0:T(8,128)S(1)}, u32[]{:S(2)}, u32[]{:S(2)}) async-start(f32[32,16,512]{2,1,0:T(8,128)} %bitcast.4), calls=%async_computation | async-start | bytes 2097152 | tf_op jit(solution)/shard_map/all_to_all | solution.py:255
  14.3 0.0 copy-start.2
  14.3 17.0 %all-to-all-done = f32[32,16,512]{2,1,0:T(8,128)S(1)} async-done(((f32[32,16,512]{2,1,0:T(8,128)}), f32[32,16,512]{2,1,0:T(8,128)S(1)}, u32[]{:S(2)}, u32[]{:S(2)}) %all-to-all-start) | async-done | bytes 1048608 | tf_op jit(solution)/shard_map/all_to_all | solution.py:255
  31.3 0.0 copy-done.2
  31.3 2.4 %shard_map.51 = f32[4,16,512]{2,1,0:T(8,128)S(1)} custom-call(s32[1]{0:T(128)} %bitcast.2.pos_ref, f32[512,512]{1,0:T(8,128)S(1)} %bitcast.9, s32[1,2048]{1,0:T(1,128)S(1)} %bitcast.10), custom_call_target="tpu_custom_call" | custom-call | tf_op jit(solution)/shard_map/pallas_call | solution.py:244
  33.8 8.3 %all_to_all.30 = f32[4,16,512]{2,1,0:T(8,128)S(1)} all-to-all(f32[4,16,512]{2,1,0:T(8,128)S(1)} %shard_map.51), channel_id=1, replica_groups=mesh['x_hi'=2,'z_hi'=4,'z_lo'=4,'x_lo'=2,'y'=4,'core'=2] {'z_lo'}, dimensions={0} | all-to-all | bytes 262144 | tf_op jit(solution)/shard_map/all_to_all | solution.py:255
  42.1 24.1 %all_to_all.31 = f32[4,16,512]{2,1,0:T(8,128)S(1)} all-to-all(f32[4,16,512]{2,1,0:T(8,128)S(1)} %broadcast_in_dim.8), channel_id=1, replica_groups=mesh['x_hi'=2,'z_hi'=4,'z_lo'=4,'x_lo'=2,'y'=4,'core'=2] {'z_hi'}, dimensions={0} | all-to-all | bytes 262144 | tf_op jit(solution)/shard_map/all_to_all | solution.py:255
  66.2 1.1 broadcast_in_dim.9
  67.3 8.0 %all-to-all-start.3 = ((f32[32,16,512]{2,1,0:T(8,128)}), f32[32,16,512]{2,1,0:T(8,128)S(1)}, u32[]{:S(2)}, u32[]{:S(2)}) async-start(f32[32,16,512]{2,1,0:T(8,128)} %broadcast_in_dim.9), calls=%async_computation.3 | async-start | bytes 2097152 | tf_op jit(solution)/shard_map/all_to_all | solution.py:255
  75.4 0.1 pad_add_fusion.place_ref
  75.5 16.9 %all-to-all-done.3 = f32[32,16,512]{2,1,0:T(8,128)S(1)} async-done(((f32[32,16,512]{2,1,0:T(8,128)}), f32[32,16,512]{2,1,0:T(8,128)S(1)}, u32[]{:S(2)}, u32[]{:S(2)}) %all-to-all-start.3) | async-done | bytes 1048608 | tf_op jit(solution)/shard_map/all_to_all | solution.py:255
  92.4 1.3 shard_map.52
  93.6 7.1 %all_to_all.32 = f32[4,40,128]{2,1,0:T(8,128)S(1)} all-to-all(f32[4,40,128]{2,1,0:T(8,128)S(1)} %broadcast_in_dim.10), channel_id=1, replica_groups=mesh['x_hi'=2,'z_hi'=4,'z_lo'=4,'x_lo'=2,'y'=4,'core'=2] {'z_lo'}, dimensions={0} | all-to-all | bytes 163840 | tf_op jit(solution)/shard_map/all_to_all | solution.py:255
  100.8 0.0 copy-start.1
  100.8 18.1 %all_to_all.33.g_ref = f32[32,40,128]{2,1,0:T(8,128)S(1)} all-to-all(f32[32,40,128]{2,1,0:T(8,128)S(1)} %broadcast_in_dim.11), channel_id=1, replica_groups=mesh['x_hi'=2,'z_hi'=4,'z_lo'=4,'x_lo'=2,'y'=4,'core'=2] {'x_hi','x_lo',..., dimensions={0} | all-to-all | bytes 1310720 | tf_op jit(solution)/shard_map/all_to_all | solution.py:255
  119.0 0.0 copy-done.1
  119.0 14.3 %shard_map.53 = (f32[512,512]{1,0:T(8,128)}, f32[512,512]{1,0:T(8,128)}) custom-call(f32[32,40,128]{2,1,0:T(8,128)S(1)} %all_to_all.33.g_ref, f32[512,512]{1,0:T(8,128)S(1)} %copy-done.1), custom_call_target="tpu_custom_call" | custom-call | tf_op jit(solution)/shard_map/pallas_call | solution.py:155
  (7 shorter events, 0.1 us)
Async XLA Ops:
  0.6 1.2 copy-start
  1.9 0.7 copy-start.3
  3.8 27.5 %all-to-all-start = ((f32[32,16,512]{2,1,0:T(8,128)}), f32[32,16,512]{2,1,0:T(8,128)S(1)}, u32[]{:S(2)}, u32[]{:S(2)}) async-start(f32[32,16,512]{2,1,0:T(8,128)} %bitcast.4), calls=%async_computation | async-start | bytes 2097152 | tf_op jit(solution)/shard_map/all_to_all | solution.py:255
  14.3 17.0 %copy-start.2 = (s32[2048]{0:T(1024)S(1)}, s32[2048]{0:T(1024)}, u32[]{:S(2)}) copy-start(s32[2048]{0:T(1024)} %param.5) | copy-start | bytes 24580
  67.3 25.0 %all-to-all-start.3 = ((f32[32,16,512]{2,1,0:T(8,128)}), f32[32,16,512]{2,1,0:T(8,128)S(1)}, u32[]{:S(2)}, u32[]{:S(2)}) async-start(f32[32,16,512]{2,1,0:T(8,128)} %broadcast_in_dim.9), calls=%async_computation.3 | async-start | bytes 2097152 | tf_op jit(solution)/shard_map/all_to_all | solution.py:255
  100.8 18.2 %copy-start.1 = (f32[512,512]{1,0:T(8,128)S(1)}, f32[512,512]{1,0:T(8,128)}, u32[]{:S(2)}) copy-start(f32[512,512]{1,0:T(8,128)} %x_ref.3) | copy-start | bytes 3145732

commit v3 on v2

--- a/solution.py
+++ b/solution.py
@@ -10,10 +10,12 @@
 CHUNK = 512
 ROW_AXES = ("x_hi", "z_hi", "z_lo", "x_lo", "y", "core")
 PLANE = ("x_hi", "x_lo", "y", "core")
+CHIPS = ("x_hi", "x_lo", "y")
 LOWER = ((0, 0), (1, 0), (1, 1), (2, 0), (2, 1), (2, 2), (3, 0), (3, 1), (3, 2), (3, 3))
 VMEM = pl.BlockSpec(memory_space=pltpu.VMEM)
 SMEM = pl.BlockSpec(memory_space=pltpu.SMEM)
 PARAMS = pltpu.CompilerParams(vmem_limit_bytes=32 * 1024 * 1024)
+WIDE = pltpu.CompilerParams(vmem_limit_bytes=60 * 1024 * 1024)
 
 
 def split2(x):
@@ -145,9 +147,8 @@
 
 
 def lower_block(g_ref, i, j):
-    core, slot = divmod(LOWER.index((i, j)), len(LOWER) // 2)
-    parts = [g_ref[chip * 2 + core, slot * 8 : slot * 8 + 8, :] for chip in range(BLOCK // 8)]
-    return jnp.concatenate(parts, axis=0)
+    first = LOWER.index((i, j)) * 8
+    return jnp.concatenate([g_ref[chip, first : first + 8, :] for chip in range(BLOCK // 8)], axis=0)
 
 
 def chol_solve(parts, x):
@@ -162,41 +163,77 @@
     )(parts, x)
 
 
-def gram_kernel(place_ref, p_ref, o_ref, split_ref):
+def gram_kernel(place_ref, own_ref, other_ref, o_ref, all_ref, split_ref):
     chip, core = place_ref[0], place_ref[1]
-    half = len(LOWER) // 2
-    split_ref[...] = right(p_ref[...])
-    for slot in range(half):
-        i = jnp.where(core == 0, LOWER[slot][0], LOWER[slot + half][0])
-        j = jnp.where(core == 0, LOWER[slot][1], LOWER[slot + half][1])
-        rows = p_ref[pl.ds(pl.multiple_of(i * BLOCK + chip * 8, 8), 8), :]
-        cols = split_ref[pl.ds(pl.multiple_of(j * BLOCK, BLOCK), BLOCK), :]
-        o_ref[slot * 8 : slot * 8 + 8, :] = dot_t(left(rows), cols)
-
-
-def gram_part(columns, place):
-    n, depth = columns.shape
+    half = own_ref.shape[0]
+    for ref, place in ((own_ref, core), (other_ref, 1 - core)):
+        at = pl.ds(pl.multiple_of(place * half, half), half)
+        all_ref[at, :] = ref[...]
+        split_ref[at, :] = right(ref[...])
+    for i in range(2 * half // BLOCK):
+        width = (i + 1) * BLOCK
+        rows = left(all_ref[pl.ds(pl.multiple_of(i * BLOCK + chip * 8, 8), 8), :])
+        product = dot_t(rows, split_ref[:width, :])
+        for j in range(i + 1):
+            first = LOWER.index((i, j)) * 8
+            o_ref[first : first + 8, :] = product[:, j * BLOCK : (j + 1) * BLOCK]
+
+
+def gram_part(own, other, place):
+    half, depth = own.shape
     return pl.pallas_call(
         gram_kernel,
-        out_shape=jax.ShapeDtypeStruct((4 * len(LOWER), BLOCK), jnp.float32),
-        in_specs=[SMEM, VMEM],
+        out_shape=jax.ShapeDtypeStruct((8 * len(LOWER), BLOCK), jnp.float32),
+        in_specs=[SMEM, VMEM, VMEM],
         out_specs=VMEM,
-        scratch_shapes=[pltpu.VMEM((n, 3 * depth), jnp.bfloat16)],
+        scratch_shapes=[
+            pltpu.VMEM((2 * half, depth), jnp.float32),
+            pltpu.VMEM((2 * half, 3 * depth), jnp.bfloat16),
+        ],
         compiler_params=PARAMS,
-    )(place, columns)
-
-
-def flip_kernel(x_ref, signs_ref, o_ref):
-    o_ref[...] = x_ref[...].T * signs_ref[...].astype(jnp.float32)
+    )(place, own, other)
+
+
+def flip_kernel(x_ref, signs_ref, o_ref, buf_ref, row_ref, sems):
+    rows, n = buf_ref.shape
+    parts = rows // BLOCK
+    group = n // 32
+    sign_copy = pltpu.make_async_copy(signs_ref, row_ref, sems.at[parts])
+    copies = []
+    for k in range(parts):
+        at = pl.ds(k * BLOCK, BLOCK)
+        copies.append(pltpu.make_async_copy(x_ref.at[at, :], buf_ref.at[at, :], sems.at[k]))
+    copies[0].start()
+    sign_copy.start()
+    for copy in copies[1:]:
+        copy.start()
+    sign_copy.wait()
+    for k in range(parts):
+        copies[k].wait()
+        at = slice(k * BLOCK, (k + 1) * BLOCK)
+        sign = row_ref[:, at].astype(jnp.float32)
+        for c in range(n // BLOCK):
+            block = buf_ref[at, c * BLOCK : (c + 1) * BLOCK].T * sign
+            for q in range(BLOCK // group):
+                core, chip = divmod(c * (BLOCK // group) + q, 16)
+                to = (2 * chip + core) * group
+                o_ref[to : to + group, at] = block[q * group : (q + 1) * group, :]
 
 
 def signed_columns(matrix, signs):
+    rows, n = matrix.shape
+    hbm = pl.BlockSpec(memory_space=pl.ANY)
     return pl.pallas_call(
         flip_kernel,
-        out_shape=jax.ShapeDtypeStruct(matrix.shape[::-1], jnp.float32),
-        in_specs=[VMEM, VMEM],
+        out_shape=jax.ShapeDtypeStruct((n, rows), jnp.float32),
+        in_specs=[hbm, hbm],
         out_specs=VMEM,
-        compiler_params=PARAMS,
+        scratch_shapes=[
+            pltpu.VMEM((rows, n), jnp.float32),
+            pltpu.VMEM((1, rows), jnp.int32),
+            pltpu.SemaphoreType.DMA((rows // BLOCK + 1,)),
+        ],
+        compiler_params=WIDE,
     )(matrix, signs.reshape(1, -1))
 
 
@@ -263,15 +300,15 @@
 def body(matrix, signs, samples):
     rows, n = matrix.shape
     plane = lax.axis_size(PLANE)
-    place = lax.axis_index(PLANE)
     columns = exchange(signed_columns(matrix, signs).reshape(plane, n // plane, rows), PLANE)
     partial = sample_columns(columns.reshape(n, rows), samples, lax.axis_index(("z_hi", "z_lo")))
     mine = jnp.sum(exchange(partial, "z_lo"), axis=0)
     mine = jnp.sum(gather(mine, "z_hi"), axis=0)
-    every = gather(mine, PLANE).reshape(n, -1)
-    part = gram_part(every, jnp.stack([place // 2, place % 2]))
+    own = gather(mine, CHIPS).reshape(n // 2, -1)
+    other = lax.ppermute(own, "core", [(0, 1), (1, 0)])
+    part = gram_part(own, other, jnp.stack([lax.axis_index(CHIPS), lax.axis_index("core")]))
     part = jnp.sum(gather(part, "z_lo"), axis=0) / jnp.float32(samples.shape[0])
-    return chol_solve(gather(part, PLANE), matrix)
+    return chol_solve(gather(part, CHIPS), matrix)
 
 
 def solution(mesh):

time: 134 us -> 126 us (0.940)
  waiting for transfers between devices: 33.9 us -> 18.4 us
  blocking collectives: 57.7 us -> 67.3 us
  local copies, waits for them, and re-layouts: 3.09 us -> 0.16 us
  Pallas kernels: 19.3 us -> 21.2 us
    all_to_all x2 -> x1, waiting for transfers between devices: 33.9 us -> 17 us  [exchange(): return lax.all_to_all(block, axes, 0, 0, tiled=True)]
    all_to_all x4 -> x5, blocking collectives: 57.7 us -> 67.3 us  [exchange(): return lax.all_to_all(block, axes, 0, 0, tiled=True)]
    all_to_all x2 -> x1, starting transfers between devices: 18.5 us -> 10.5 us  [exchange(): return lax.all_to_all(block, axes, 0, 0, tiled=True)]
    ppermute x0 -> x1, starting transfers between devices: none -> 6.78 us  [body(): other = lax.ppermute(own, 'core', [(0, 1), (1, 0)])]
    pallas_call x2, Pallas kernels: 2.56 us -> 4.47 us  [the longest x1 2.51 us: signed_columns(): pl.pallas_call(flip_kernel, out_shape=jax.ShapeDtypeStruct((n, rows), jnp...]
    unnamed x8 -> x4, local copies, waits for them, and re-layouts: 1.91 us -> 0.01 us
    ppermute x0 -> x1, waiting for transfers between devices: none -> 1.43 us  [body(): other = lax.ppermute(own, 'core', [(0, 1), (1, 0)])]
where the time goes in v3:
time: 126 us; the launch traced here: 125 us
  blocking collectives  67.3 us (53%)
  Pallas kernels  21.2 us (17%)
  waiting for transfers between devices  18.4 us (15%)
  starting transfers between devices  17.3 us (14%)
    all_to_all x5, blocking collectives, exchange(): return lax.all_to_all(block, axes, 0, 0, tiled=True)  67.3 us
    all_to_all x1, waiting for transfers between devices, exchange(): return lax.all_to_all(block, axes, 0, 0, tiled=True)  17 us
    pallas_call x1, Pallas kernels, chol_solve(): pl.pallas_call(chol_kernel, out_shape=(jax.ShapeDtypeStruct((n, n), jnp.f...  14.3 us
    all_to_all x1, starting transfers between devices, exchange(): return lax.all_to_all(block, axes, 0, 0, tiled=True)  10.5 us
    ppermute x1, starting transfers between devices, body(): other = lax.ppermute(own, 'core', [(0, 1), (1, 0)])  6.78 us
  transfers between devices with their start and end apart: 2, of which 2 were waited for; matrix products, arithmetic and copies ran while one was open for 0% of the time, Pallas kernels for 0%

profile of v3, /device:TPU:1, one launch (start us, length us, event | category | flops | bytes accessed | tf_op | source)
XLA Modules:
  0.0 125.2 jit_solution(17889406958612063625)
XLA Ops:
  0.6 2.5 %shard_map.50 = f32[512,512]{1,0:T(8,128)} custom-call(f32[512,512]{1,0:T(8,128)} %x_ref.3, s32[1,512]{1,0:T(1,128)} %bitcast.13), custom_call_target="tpu_custom_call" | custom-call | tf_op jit(solution)/shard_map/pallas_call | solution.py:226
  3.1 10.5 %all-to-all-start = ((f32[32,16,512]{2,1,0:T(8,128)}), f32[32,16,512]{2,1,0:T(8,128)S(1)}, u32[]{:S(2)}, u32[]{:S(2)}) async-start(f32[32,16,512]{2,1,0:T(8,128)} %bitcast.12), calls=%async_computation | async-start | bytes 2097152 | tf_op jit(solution)/shard_map/all_to_all | solution.py:292
  13.6 0.0 copy-start.1
  13.6 17.0 %all-to-all-done = f32[32,16,512]{2,1,0:T(8,128)S(1)} async-done(((f32[32,16,512]{2,1,0:T(8,128)}), f32[32,16,512]{2,1,0:T(8,128)S(1)}, u32[]{:S(2)}, u32[]{:S(2)}) %all-to-all-start) | async-done | bytes 1048608 | tf_op jit(solution)/shard_map/all_to_all | solution.py:292
  30.6 0.0 copy-done.1
  30.6 2.4 %shard_map.51 = f32[4,16,512]{2,1,0:T(8,128)S(1)} custom-call(s32[1]{0:T(128)} %bitcast.2.pos_ref, f32[512,512]{1,0:T(8,128)S(1)} %bitcast.8, s32[1,2048]{1,0:T(1,128)S(1)} %bitcast.11), custom_call_target="tpu_custom_call" | custom-call | tf_op jit(solution)/shard_map/pallas_call | solution.py:281
  33.1 8.3 %all_to_all.30 = f32[4,16,512]{2,1,0:T(8,128)S(1)} all-to-all(f32[4,16,512]{2,1,0:T(8,128)S(1)} %shard_map.51), channel_id=1, replica_groups=mesh['x_hi'=2,'z_hi'=4,'z_lo'=4,'x_lo'=2,'y'=4,'core'=2] {'z_lo'}, dimensions={0} | all-to-all | bytes 262144 | tf_op jit(solution)/shard_map/all_to_all | solution.py:292
  41.4 24.1 %all_to_all.31 = f32[4,16,512]{2,1,0:T(8,128)S(1)} all-to-all(f32[4,16,512]{2,1,0:T(8,128)S(1)} %broadcast_in_dim.8), channel_id=1, replica_groups=mesh['x_hi'=2,'z_hi'=4,'z_lo'=4,'x_lo'=2,'y'=4,'core'=2] {'z_hi'}, dimensions={0} | all-to-all | bytes 262144 | tf_op jit(solution)/shard_map/all_to_all | solution.py:292
  65.5 0.1 broadcast_in_dim.9
  65.6 12.9 %all_to_all.32 = f32[16,16,512]{2,1,0:T(8,128)S(1)} all-to-all(f32[16,16,512]{2,1,0:T(8,128)S(1)} %broadcast_in_dim.9), channel_id=1, replica_groups=mesh['x_hi'=2,'z_hi'=4,'z_lo'=4,'x_lo'=2,'y'=4,'core'=2] {'x_hi','x_lo',..., dimensions={0} | all-to-all | bytes 1048576 | tf_op jit(solution)/shard_map/all_to_all | solution.py:292
  78.5 6.8 %collective-permute-start = (f32[256,512]{1,0:T(8,128)S(1)}, f32[256,512]{1,0:T(8,128)S(1)}, u32[]{:S(2)}, u32[]{:S(2)}) collective-permute-start(f32[256,512]{1,0:T(8,128)S(1)} %bitcast.9), channel_id=1, source_target_pairs={{0,1},{1,0},{2,3},{3,2},{4,5},{5,4},{6,7},{7,6},{8,9},{9,8},{10,11... | collective-permute-start | bytes 1572872 | tf_op jit(solution)/shard_map/ppermute | solution.py:308
  85.3 0.1 pad_add_fusion.place_ref
  85.4 1.4 %collective-permute-done.other_ref = f32[256,512]{1,0:T(8,128)S(1)} collective-permute-done((f32[256,512]{1,0:T(8,128)S(1)}, f32[256,512]{1,0:T(8,128)S(1)}, u32[]{:S(2)}, u32[]{:S(2)}) %collective-permute-start) | collective-permute-done | bytes 524320 | tf_op jit(solution)/shard_map/ppermute | solution.py:308
  86.8 2.0 %shard_map.52 = f32[80,128]{1,0:T(8,128)S(1)} custom-call(s32[2]{0:T(128)S(1)} %pad_add_fusion.place_ref, f32[256,512]{1,0:T(8,128)S(1)} %bitcast.10, f32[256,512]{1,0:T(8,128)S(1)} %collective-permute-done.other_ref), custom_call_target="tpu_custom_call" | custom-call | tf_op jit(solution)/shard_map/pallas_call | solution.py:184
  88.8 8.4 %all_to_all.33 = f32[4,80,128]{2,1,0:T(8,128)S(1)} all-to-all(f32[4,80,128]{2,1,0:T(8,128)S(1)} %broadcast_in_dim.10), channel_id=1, replica_groups=mesh['x_hi'=2,'z_hi'=4,'z_lo'=4,'x_lo'=2,'y'=4,'core'=2] {'z_lo'}, dimensions={0} | all-to-all | bytes 327680 | tf_op jit(solution)/shard_map/all_to_all | solution.py:292
  97.2 0.0 copy-start
  97.3 13.6 %all_to_all.34.g_ref = f32[16,80,128]{2,1,0:T(8,128)S(1)} all-to-all(f32[16,80,128]{2,1,0:T(8,128)S(1)} %broadcast_in_dim.11), channel_id=1, replica_groups=mesh['x_hi'=2,'z_hi'=4,'z_lo'=4,'x_lo'=2,'y'=4,'core'=2] {'x_hi','x_lo',..., dimensions={0} | all-to-all | bytes 1310720 | tf_op jit(solution)/shard_map/all_to_all | solution.py:292
  110.9 0.0 copy-done
  110.9 14.3 %shard_map.53 = (f32[512,512]{1,0:T(8,128)}, f32[512,512]{1,0:T(8,128)}) custom-call(f32[16,80,128]{2,1,0:T(8,128)S(1)} %all_to_all.34.g_ref, f32[512,512]{1,0:T(8,128)S(1)} %copy-done), custom_call_target="tpu_custom_call" | custom-call | tf_op jit(solution)/shard_map/pallas_call | solution.py:156
  (7 shorter events, 0.1 us)
Async XLA Ops:
  3.1 27.5 %all-to-all-start = ((f32[32,16,512]{2,1,0:T(8,128)}), f32[32,16,512]{2,1,0:T(8,128)S(1)}, u32[]{:S(2)}, u32[]{:S(2)}) async-start(f32[32,16,512]{2,1,0:T(8,128)} %bitcast.12), calls=%async_computation | async-start | bytes 2097152 | tf_op jit(solution)/shard_map/all_to_all | solution.py:292
  13.6 17.0 %copy-start.1 = (s32[2048]{0:T(1024)S(1)}, s32[2048]{0:T(1024)}, u32[]{:S(2)}) copy-start(s32[2048]{0:T(1024)} %param.5) | copy-start | bytes 24580
  78.5 8.3 %collective-permute-start = (f32[256,512]{1,0:T(8,128)S(1)}, f32[256,512]{1,0:T(8,128)S(1)}, u32[]{:S(2)}, u32[]{:S(2)}) collective-permute-start(f32[256,512]{1,0:T(8,128)S(1)} %bitcast.9), channel_id=1, source_target_pairs={{0,1},{1,0},{2,3},{3,2},{4,5},{5,4},{6,7},{7,6},{8,9},{9,8},{10,11... | collective-permute-start | bytes 1572872 | tf_op jit(solution)/shard_map/ppermute | solution.py:308
  97.2 13.7 %copy-start = (f32[512,512]{1,0:T(8,128)S(1)}, f32[512,512]{1,0:T(8,128)}, u32[]{:S(2)}) copy-start(f32[512,512]{1,0:T(8,128)} %x_ref.3) | copy-start | bytes 3145732

commit v4 on v3

v4 whole, which is shorter than its diff:
```python
import jax
import jax.numpy as jnp
from jax import lax
from jax.experimental import pallas as pl
from jax.experimental.pallas import tpu as pltpu
from jax.sharding import Mesh
from jax.sharding import PartitionSpec as P

BLOCK = 128
CHUNK = 512
SHARE = 256
ROW_AXES = ("x_hi", "z_hi", "z_lo", "x_lo", "y", "core")
PLANE = ("x_hi", "x_lo", "y", "core")
CHIPS = ("x_hi", "x_lo", "y")
NEAR = ("z_lo", "core")
LOWER = ((0, 0), (1, 0), (1, 1), (2, 0), (2, 1), (2, 2), (3, 0), (3, 1), (3, 2), (3, 3))
VMEM = pl.BlockSpec(memory_space=pltpu.VMEM)
SMEM = pl.BlockSpec(memory_space=pltpu.SMEM)
PARAMS = pltpu.CompilerParams(vmem_limit_bytes=32 * 1024 * 1024)
WIDE = pltpu.CompilerParams(vmem_limit_bytes=60 * 1024 * 1024)


def split2(x):
    hi = x.astype(jnp.bfloat16)
    return hi, (x - hi.astype(jnp.float32)).astype(jnp.bfloat16)


def left(x):
    hi, lo = split2(x)
    return jnp.concatenate([hi, hi, lo], axis=1)


def right(x):
    hi, lo = split2(x)
    return jnp.concatenate([hi, lo, hi], axis=1)


def dot_t(a, b):
    return lax.dot_general(a, b, (((1,), (1,)), ((), ())), preferred_element_type=jnp.float32)


def factor_block(rows, c_ref, u_ref, w_ref):
    lane = lax.broadcasted_iota(jnp.int32, (8, BLOCK), 1)
    sub = lax.broadcasted_iota(jnp.int32, (8, BLOCK), 0)
    rows = list(rows)
    groups = len(rows)
    full = (8, BLOCK)
    for k in range(groups):
        base = k * 8
        own = (lane >= base) & (lane < base + 8)
        panel = rows[k]
        for j in range(8):
            c_ref[k % 2, j] = jnp.broadcast_to(panel[:, base + j : base + j + 1], full)
        c_ref[k % 2, 8] = panel
        spread = lambda j, i: jnp.broadcast_to(c_ref[k % 2, j, i : i + 1, :], full)
        piv = {(i, j): spread(j, i) for i in range(8) for j in range(i + 1)}
        root, inv, low, ratio = {}, {}, {}, {}
        for j in range(0, 8, 2):
            x, y, z = piv[j, j], piv[j + 1, j], piv[j + 1, j + 1]
            det = x * z - y * y
            rd = 1.0 / det
            for i in range(j + 2, 8):
                p, q = piv[i, j], piv[i, j + 1]
                f, g = p * z - q * y, q * x - p * y
                low[i, j], low[i, j + 1] = f * rd, g * rd
                for m in range(j + 2, i + 1):
                    if i < j + 4:
                        piv[i, m] = piv[i, m] - (f * piv[m, j] + g * piv[m, j + 1]) * rd
                    else:
                        piv[i, m] = piv[i, m] - low[i, j] * piv[m, j] - low[i, j + 1] * piv[m, j + 1]
            inv[j] = (z * rd, y * rd, x * rd)
            root[j] = lax.rsqrt(x)
            root[j + 1] = lax.rsqrt(det) * (x * root[j])
            ratio[j] = y * (root[j] * root[j])
        fwd, fwd_u = [], []
        for i in range(8):
            u = spread(8, i)
            w = jnp.where(own, jnp.where(lane == base + i, 1.0, 0.0), u)
            for j in range(i - i % 2):
                w = w - low[i, j] * fwd[j]
                u = u - low[i, j] * fwd_u[j]
            fwd.append(w)
            fwd_u.append(u)
        back = [None] * 8
        for i in reversed(range(0, 8, 2)):
            f, g = fwd[i], fwd[i + 1]
            x, y, z = inv[i]
            v, w = f * x - g * y, g * z - f * y
            for j in range(i + 2, 8):
                v = v - low[j, i] * back[j]
                w = w - low[j, i + 1] * back[j]
            back[i], back[i + 1] = v, w
        for r in range(k + 1, groups):
            terms = [jnp.broadcast_to(rows[r][:, base + j : base + j + 1], full) * back[j] for j in range(8)]
            while len(terms) > 1:
                terms = [x + y for x, y in zip(terms[::2], terms[1::2])]
            rows[r] = jnp.where(own, 0.0, rows[r]) - terms[0]
        for g in range(8):
            h = g - g % 2
            w = fwd[g] if g == h else fwd[g] - ratio[h] * fwd[h]
            u = fwd_u[g] if g == h else fwd_u[g] - ratio[h] * fwd_u[h]
            u_ref[base + g : base + g + 1, :] = jnp.where(lane >= base + g, u * root[g], 0.0)[:1, :]
            w_ref[base + g : base + g + 1, :] = jnp.where(lane <= base + g, w * root[g], 0.0)[:1, :]


def chol_kernel(g_ref, x_ref, l_out, o_out, a_ref, l_ref, o_ref, c_ref, u_ref, w_ref, sems):
    n = x_ref.shape[1]
    nb = n // BLOCK
    at = [slice(k * BLOCK, (k + 1) * BLOCK) for k in range(nb)]
    r = lax.broadcasted_iota(jnp.int32, (BLOCK, BLOCK), 0)
    c = lax.broadcasted_iota(jnp.int32, (BLOCK, BLOCK), 1)
    row_scale, col_scale, row_root = [], [], []
    copies = []
    for k in range(nb):
        diag = jnp.where(r == c, lower_block(g_ref, k, k), 0.0)
        by_row = jnp.broadcast_to(jnp.sum(diag, axis=1, keepdims=True), (BLOCK, BLOCK))
        s = lax.rsqrt(by_row)
        row_scale.append(s)
        row_root.append(by_row * s)
        col_scale.append(lax.rsqrt(jnp.sum(diag, axis=0, keepdims=True)))
    for k in range(nb):
        for i in range(k, nb):
            a_ref[at[i], at[k]] = lower_block(g_ref, i, k) * row_scale[i] * col_scale[k]
    for k in range(nb):
        panels = [a_ref[k * BLOCK + p * 8 : k * BLOCK + (p + 1) * 8, at[k]] for p in range(BLOCK // 8)]
        factor_block(panels, c_ref, u_ref.at[k % 2], w_ref.at[k % 2])
        ws = right(w_ref[k % 2])
        below = {}
        for i in range(k + 1, nb):
            below[i] = dot_t(left(a_ref[at[i], at[k]]), ws)
            for j in range(k + 1, i + 1):
                a_ref[at[i], at[j]] = a_ref[at[i], at[j]] - dot_t(left(below[i]), right(below[j]))
        before = x_ref[:, at[k]] * col_scale[k]
        if k:
            before = before - o_ref[:, at[k]]
        solved = dot_t(left(before), ws)
        o_ref[:, at[k]] = solved
        for i in range(k + 1, nb):
            add = dot_t(left(solved), right(below[i]))
            o_ref[:, at[i]] = o_ref[:, at[i]] + add if k else add
        for i in range(k):
            l_ref[at[i], at[k]] = jnp.zeros((BLOCK, BLOCK), jnp.float32)
        l_ref[at[k], at[k]] = u_ref[k % 2].T * row_root[k]
        for i in range(k + 1, nb):
            l_ref[at[i], at[k]] = below[i] * row_root[i]
        copies.append(pltpu.make_async_copy(o_ref.at[:, at[k]], o_out.at[:, at[k]], sems.at[2 * k]))
        copies.append(pltpu.make_async_copy(l_ref.at[:, at[k]], l_out.at[:, at[k]], sems.at[2 * k + 1]))
        copies[-2].start()
        copies[-1].start()
    for copy in copies:
        copy.wait()


def lower_block(g_ref, i, j):
    first = LOWER.index((i, j)) * 8
    return jnp.concatenate([g_ref[chip, first : first + 8, :] for chip in range(BLOCK // 8)], axis=0)


def chol_solve(parts, x):
    rows, n = x.shape
    return pl.pallas_call(
        chol_kernel,
        out_shape=(jax.ShapeDtypeStruct((n, n), jnp.float32), jax.ShapeDtypeStruct(x.shape, jnp.float32)),
        in_specs=[VMEM, VMEM],
        out_specs=[pl.BlockSpec(memory_space=pl.ANY)] * 2,
        scratch_shapes=[
            pltpu.VMEM((n, n), jnp.float32),
            pltpu.VMEM((n, n), jnp.float32),
            pltpu.VMEM((rows, n), jnp.float32),
            pltpu.VMEM((2, 9, 8, BLOCK), jnp.float32),
            pltpu.VMEM((2, BLOCK, BLOCK), jnp.float32),
            pltpu.VMEM((2, BLOCK, BLOCK), jnp.float32),
            pltpu.SemaphoreType.DMA((2 * (n // BLOCK),)),
        ],
        compiler_params=PARAMS,
    )(parts, x)


def gram_kernel(chip_ref, p_ref, o_ref):
    blocks = p_ref.shape[0] // BLOCK
    first = chip_ref[0] * 8
    rows = [p_ref[pl.ds(pl.multiple_of(i * BLOCK + first, 8), 8), :] for i in range(blocks)]
    product = dot_t(left(jnp.concatenate(rows, axis=0)), right(p_ref[...]))
    for t, (i, j) in enumerate(LOWER):
        o_ref[t * 8 : t * 8 + 8, :] = product[i * 8 : i * 8 + 8, j * BLOCK : (j + 1) * BLOCK]


def gram_part(columns, chip):
    return pl.pallas_call(
        gram_kernel,
        out_shape=jax.ShapeDtypeStruct((8 * len(LOWER), BLOCK), jnp.float32),
        in_specs=[SMEM, VMEM],
        out_specs=VMEM,
        compiler_params=PARAMS,
    )(chip.reshape(1), columns)


def flip_kernel(x_ref, signs_ref, o_ref, buf_ref, row_ref, sems):
    rows, n = buf_ref.shape
    parts = rows // BLOCK
    sign_copy = pltpu.make_async_copy(signs_ref, row_ref, sems.at[parts])
    copies = []
    for k in range(parts):
        at = pl.ds(k * BLOCK, BLOCK)
        copies.append(pltpu.make_async_copy(x_ref.at[at, :], buf_ref.at[at, :], sems.at[k]))
    copies[0].start()
    sign_copy.start()
    for copy in copies[1:]:
        copy.start()
    sign_copy.wait()
    for k in range(parts):
        copies[k].wait()
        at = slice(k * BLOCK, (k + 1) * BLOCK)
        sign = row_ref[:, at].astype(jnp.float32)
        for c in range(n // BLOCK):
            cols = slice(c * BLOCK, (c + 1) * BLOCK)
            o_ref[cols, at] = buf_ref[at, cols].T * sign


def signed_columns(matrix, signs):
    rows, n = matrix.shape
    hbm = pl.BlockSpec(memory_space=pl.ANY)
    return pl.pallas_call(
        flip_kernel,
        out_shape=jax.ShapeDtypeStruct((n, rows), jnp.float32),
        in_specs=[hbm, hbm],
        out_specs=VMEM,
        scratch_shapes=[
            pltpu.VMEM((rows, n), jnp.float32),
            pltpu.VMEM((1, rows), jnp.int32),
            pltpu.SemaphoreType.DMA((rows // BLOCK + 1,)),
        ],
        compiler_params=WIDE,
    )(matrix, signs.reshape(1, -1))


def signs_of(value, count):
    v = lax.broadcasted_iota(jnp.int32, (count, value.shape[1]), 0) & value
    for shift in (4, 2, 1):
        v = v ^ (v >> shift)
    return (1 - 2 * (v & 1)).astype(jnp.float32)


def mix_kernel(pos_ref, x_ref, samples_ref, o_ref, h_ref):
    width = x_ref.shape[0]
    depth = x_ref.shape[1]
    sources = 32
    cols = width // sources
    hi, lo = split2(x_ref[...])
    z_bits = pos_ref[0]
    scale = 1.0 / 512.0
    for c in range(samples_ref.shape[1] // CHUNK):
        s = samples_ref[:, c * CHUNK : (c + 1) * CHUNK]
        within = s & (depth - 1)
        device = s // depth
        low = signs_of(within & 15, 16)
        high = signs_of(within // 16, depth // 16)
        for r in range(depth // 16):
            h_ref[r * 16 : (r + 1) * 16, :] = (low * high[r : r + 1, :]).astype(jnp.bfloat16)
        plane_sign = signs_of((device & 15) | ((device // 256) * 16), sources)
        zv = (device // 16) & z_bits
        zv = zv ^ (zv >> 2)
        zv = zv ^ (zv >> 1)
        z_sign = (1 - 2 * (zv & 1)).astype(jnp.float32) * scale
        h = h_ref[...]
        t = jnp.dot(hi, h, preferred_element_type=jnp.float32)
        t = t + jnp.dot(lo, h, preferred_element_type=jnp.float32)
        acc = t[:cols, :]
        for p in range(1, sources):
            acc = acc + t[p * cols : (p + 1) * cols, :] * plane_sign[p : p + 1, :]
        acc = acc * z_sign
        for b in range(CHUNK // SHARE):
            o_ref[c * (CHUNK // SHARE) + b] = acc[:, b * SHARE : (b + 1) * SHARE]


def sample_columns(columns, samples, z_index):
    width = columns.shape[0]
    count = samples.shape[0]
    return pl.pallas_call(
        mix_kernel,
        out_shape=jax.ShapeDtypeStruct((count // SHARE, width // 32, SHARE), jnp.float32),
        in_specs=[SMEM, VMEM, VMEM],
        out_specs=VMEM,
        scratch_shapes=[pltpu.VMEM((columns.shape[1], CHUNK), jnp.bfloat16)],
        compiler_params=PARAMS,
    )(z_index.reshape(1), columns, samples.reshape(1, count))


def exchange(block, axes):
    return lax.all_to_all(block, axes, 0, 0, tiled=True)


def gather(block, axes):
    count = lax.axis_size(axes)
    return exchange(jnp.broadcast_to(block[None], (count,) + block.shape), axes)


def body(matrix, signs, samples):
    rows, n = matrix.shape
    plane = lax.axis_size(PLANE)
    columns = exchange(signed_columns(matrix, signs).reshape(plane, n // plane, rows), PLANE)
    partial = sample_columns(columns.reshape(n, rows), samples, lax.axis_index(("z_hi", "z_lo")))
    mine = exchange(partial, NEAR).reshape(lax.axis_size("z_lo"), 2 * (n // plane), -1)
    mine = jnp.sum(gather(jnp.sum(mine, axis=0), "z_hi"), axis=0)
    every = gather(mine, CHIPS).reshape(n, -1)
    part = gram_part(every, lax.axis_index(CHIPS))
    part = jnp.sum(gather(part, NEAR), axis=0) / jnp.float32(samples.shape[0])
    return chol_solve(gather(part, CHIPS), matrix)


def solution(mesh):
    fine = Mesh(mesh.devices.reshape(2, 4, 4, 2, 4, 2), ROW_AXES)
    in_specs = (P(ROW_AXES, None), P(ROW_AXES), P())
    out_specs = (P(), P(ROW_AXES, None))
    return jax.shard_map(body, mesh=fine, in_specs=in_specs, out_specs=out_specs, check_vma=False)
```

time: 126 us -> 129 us (1.024)
  waiting for transfers between devices: 18.4 us -> 25.9 us
  starting transfers between devices: 17.3 us -> 14 us
  Pallas kernels: 21.2 us -> 19.2 us
    all_to_all x1 -> x2, waiting for transfers between devices: 17 us -> 25.9 us  [exchange(): return lax.all_to_all(block, axes, 0, 0, tiled=True)]
    ppermute x1 -> x0, starting transfers between devices: 6.78 us -> none  [body(): other = lax.ppermute(own, 'core', [(0, 1), (1, 0)])]
    all_to_all x1 -> x2, starting transfers between devices: 10.5 us -> 14 us  [exchange(): return lax.all_to_all(block, axes, 0, 0, tiled=True)]
    pallas_call x1, Pallas kernels: 1.96 us -> 0.3 us  [gram_part(): pl.pallas_call(gram_kernel, out_shape=jax.ShapeDtypeStruct((8 * len(LOWER...]
    ppermute x1 -> x0, waiting for transfers between devices: 1.43 us -> none  [body(): other = lax.ppermute(own, 'core', [(0, 1), (1, 0)])]
    all_to_all x5 -> x4, blocking collectives: 67.3 us -> 67.4 us  [exchange(): return lax.all_to_all(block, axes, 0, 0, tiled=True)]
where the time goes in v4:
time: 129 us; the launch traced here: 128 us
  blocking collectives  67.4 us (52%)
  waiting for transfers between devices  25.9 us (20%)
  Pallas kernels  19.2 us (15%)
  starting transfers between devices  14 us (11%)
    all_to_all x4, blocking collectives, exchange(): return lax.all_to_all(block, axes, 0, 0, tiled=True)  67.4 us
    all_to_all x2, waiting for transfers between devices, exchange(): return lax.all_to_all(block, axes, 0, 0, tiled=True)  25.9 us
    all_to_all x2, starting transfers between devices, exchange(): return lax.all_to_all(block, axes, 0, 0, tiled=True)  14 us
    pallas_call x1, Pallas kernels, chol_solve(): pl.pallas_call(chol_kernel, out_shape=(jax.ShapeDtypeStruct((n, n), jnp.f...  14 us
  transfers between devices with their start and end apart: 2, of which 2 were waited for; matrix products, arithmetic and copies ran while one was open for 0% of the time, Pallas kernels for 0%

profile of v4, /device:TPU:1, one launch (start us, length us, event | category | flops | bytes accessed | tf_op | source)
XLA Modules:
  0.0 128.4 jit_solution(14328607862860946388)
XLA Ops:
  0.6 2.5 %shard_map.50 = f32[512,512]{1,0:T(8,128)} custom-call(f32[512,512]{1,0:T(8,128)} %x_ref.3, s32[1,512]{1,0:T(1,128)} %bitcast.15), custom_call_target="tpu_custom_call" | custom-call | tf_op jit(solution)/shard_map/pallas_call | solution.py:223
  3.1 10.5 %all-to-all-start = ((f32[32,16,512]{2,1,0:T(8,128)}), f32[32,16,512]{2,1,0:T(8,128)S(1)}, u32[]{:S(2)}, u32[]{:S(2)}) async-start(f32[32,16,512]{2,1,0:T(8,128)} %bitcast.13), calls=%async_computation | async-start | bytes 2097152 | tf_op jit(solution)/shard_map/all_to_all | solution.py:290
  13.6 0.0 copy-start.1
  13.6 17.0 %all-to-all-done = f32[32,16,512]{2,1,0:T(8,128)S(1)} async-done(((f32[32,16,512]{2,1,0:T(8,128)}), f32[32,16,512]{2,1,0:T(8,128)S(1)}, u32[]{:S(2)}, u32[]{:S(2)}) %all-to-all-start) | async-done | bytes 1048608 | tf_op jit(solution)/shard_map/all_to_all | solution.py:290
  30.6 0.0 copy-done.1
  30.6 2.4 %shard_map.51 = f32[8,16,256]{2,1,0:T(8,128)S(1)} custom-call(s32[1]{0:T(128)} %bitcast.1.pos_ref, f32[512,512]{1,0:T(8,128)S(1)} %bitcast.10, s32[1,2048]{1,0:T(1,128)S(1)} %bitcast.12), custom_call_target="tpu_custom_call" | custom-call | tf_op jit(solution)/shard_map/pallas_call | solution.py:279
  33.1 9.7 %all_to_all.30 = f32[8,16,256]{2,1,0:T(8,128)S(1)} all-to-all(f32[8,16,256]{2,1,0:T(8,128)S(1)} %shard_map.51), channel_id=1, replica_groups=mesh['x_hi'=2,'z_hi'=4,'z_lo'=4,'x_lo'=2,'y'=4,'core'=2] {'z_lo','core'}, dimensions={0} | all-to-all | bytes 262144 | tf_op jit(solution)/shard_map/all_to_all | solution.py:290
  42.8 24.7 %all_to_all.31 = f32[4,32,256]{2,1,0:T(8,128)S(1)} all-to-all(f32[4,32,256]{2,1,0:T(8,128)S(1)} %broadcast_in_dim.8), channel_id=1, replica_groups=mesh['x_hi'=2,'z_hi'=4,'z_lo'=4,'x_lo'=2,'y'=4,'core'=2] {'z_hi'}, dimensions={0} | all-to-all | bytes 262144 | tf_op jit(solution)/shard_map/all_to_all | solution.py:290
  67.5 0.8 broadcast_in_dim.9
  68.3 3.6 %all-to-all-start.3 = ((f32[16,32,256]{2,1,0:T(8,128)}), f32[16,32,256]{2,1,0:T(8,128)S(1)}, u32[]{:S(2)}, u32[]{:S(2)}) async-start(f32[16,32,256]{2,1,0:T(8,128)} %broadcast_in_dim.9), calls=%async_computation.3 | async-start | bytes 1048576 | tf_op jit(solution)/shard_map/all_to_all | solution.py:290
  71.9 8.9 %all-to-all-done.3 = f32[16,32,256]{2,1,0:T(8,128)S(1)} async-done(((f32[16,32,256]{2,1,0:T(8,128)}), f32[16,32,256]{2,1,0:T(8,128)S(1)}, u32[]{:S(2)}, u32[]{:S(2)}) %all-to-all-start.3) | async-done | bytes 524320 | tf_op jit(solution)/shard_map/all_to_all | solution.py:290
  80.8 0.3 shard_map.52
  81.1 0.1 broadcast_in_dim.10
  81.2 18.3 %all_to_all.32 = f32[8,80,128]{2,1,0:T(8,128)S(1)} all-to-all(f32[8,80,128]{2,1,0:T(8,128)S(1)} %broadcast_in_dim.10), channel_id=1, replica_groups=mesh['x_hi'=2,'z_hi'=4,'z_lo'=4,'x_lo'=2,'y'=4,'core'=2] {'z_lo','core'}, dimensions={0} | all-to-all | bytes 655360 | tf_op jit(solution)/shard_map/all_to_all | solution.py:290
  99.6 0.0 copy-start
  99.6 14.7 %all_to_all.33.g_ref = f32[16,80,128]{2,1,0:T(8,128)S(1)} all-to-all(f32[16,80,128]{2,1,0:T(8,128)S(1)} %broadcast_in_dim.11), channel_id=1, replica_groups=mesh['x_hi'=2,'z_hi'=4,'z_lo'=4,'x_lo'=2,'y'=4,'core'=2] {'x_hi','x_lo',..., dimensions={0} | all-to-all | bytes 1310720 | tf_op jit(solution)/shard_map/all_to_all | solution.py:290
  114.3 0.0 copy-done
  114.3 14.0 %shard_map.53 = (f32[512,512]{1,0:T(8,128)}, f32[512,512]{1,0:T(8,128)}) custom-call(f32[16,80,128]{2,1,0:T(8,128)S(1)} %all_to_all.33.g_ref, f32[512,512]{1,0:T(8,128)S(1)} %copy-done), custom_call_target="tpu_custom_call" | custom-call | tf_op jit(solution)/shard_map/pallas_call | solution.py:161
  (6 shorter events, 0.1 us)
Async XLA Ops:
  3.1 27.5 %all-to-all-start = ((f32[32,16,512]{2,1,0:T(8,128)}), f32[32,16,512]{2,1,0:T(8,128)S(1)}, u32[]{:S(2)}, u32[]{:S(2)}) async-start(f32[32,16,512]{2,1,0:T(8,128)} %bitcast.13), calls=%async_computation | async-start | bytes 2097152 | tf_op jit(solution)/shard_map/all_to_all | solution.py:290
  13.6 17.0 %copy-start.1 = (s32[2048]{0:T(1024)S(1)}, s32[2048]{0:T(1024)}, u32[]{:S(2)}) copy-start(s32[2048]{0:T(1024)} %param.5) | copy-start | bytes 24580
  68.3 12.5 %all-to-all-start.3 = ((f32[16,32,256]{2,1,0:T(8,128)}), f32[16,32,256]{2,1,0:T(8,128)S(1)}, u32[]{:S(2)}, u32[]{:S(2)}) async-start(f32[16,32,256]{2,1,0:T(8,128)} %broadcast_in_dim.9), calls=%async_computation.3 | async-start | bytes 1048576 | tf_op jit(solution)/shard_map/all_to_all | solution.py:290
  99.6 14.7 %copy-start = (f32[512,512]{1,0:T(8,128)S(1)}, f32[512,512]{1,0:T(8,128)}, u32[]{:S(2)}) copy-start(f32[512,512]{1,0:T(8,128)} %x_ref.3) | copy-start | bytes 3145732

commit v5 on v4

--- a/solution.py
+++ b/solution.py
@@ -10,7 +10,6 @@
 CHUNK = 512
 SHARE = 256
 ROW_AXES = ("x_hi", "z_hi", "z_lo", "x_lo", "y", "core")
-PLANE = ("x_hi", "x_lo", "y", "core")
 CHIPS = ("x_hi", "x_lo", "y")
 NEAR = ("z_lo", "core")
 LOWER = ((0, 0), (1, 0), (1, 1), (2, 0), (2, 1), (2, 2), (3, 0), (3, 1), (3, 2), (3, 3))
@@ -103,7 +102,7 @@
             w_ref[base + g : base + g + 1, :] = jnp.where(lane <= base + g, w * root[g], 0.0)[:1, :]
 
 
-def chol_kernel(g_ref, x_ref, l_out, o_out, a_ref, l_ref, o_ref, c_ref, u_ref, w_ref, sems):
+def chol_kernel(core_ref, own_ref, other_ref, x_ref, l_out, o_out, a_ref, l_ref, o_ref, c_ref, u_ref, w_ref, sems):
     n = x_ref.shape[1]
     nb = n // BLOCK
     at = [slice(k * BLOCK, (k + 1) * BLOCK) for k in range(nb)]
@@ -111,8 +110,9 @@
     c = lax.broadcasted_iota(jnp.int32, (BLOCK, BLOCK), 1)
     row_scale, col_scale, row_root = [], [], []
     copies = []
+    gram = lambda i, j: lower_block(core_ref[0], own_ref, other_ref, i, j)
     for k in range(nb):
-        diag = jnp.where(r == c, lower_block(g_ref, k, k), 0.0)
+        diag = jnp.where(r == c, gram(k, k), 0.0)
         by_row = jnp.broadcast_to(jnp.sum(diag, axis=1, keepdims=True), (BLOCK, BLOCK))
         s = lax.rsqrt(by_row)
         row_scale.append(s)
@@ -120,7 +120,7 @@
         col_scale.append(lax.rsqrt(jnp.sum(diag, axis=0, keepdims=True)))
     for k in range(nb):
         for i in range(k, nb):
-            a_ref[at[i], at[k]] = lower_block(g_ref, i, k) * row_scale[i] * col_scale[k]
+            a_ref[at[i], at[k]] = gram(i, k) * row_scale[i] * col_scale[k]
     for k in range(nb):
         panels = [a_ref[k * BLOCK + p * 8 : k * BLOCK + (p + 1) * 8, at[k]] for p in range(BLOCK // 8)]
         factor_block(panels, c_ref, u_ref.at[k % 2], w_ref.at[k % 2])
@@ -151,17 +151,20 @@
         copy.wait()
 
 
-def lower_block(g_ref, i, j):
-    first = LOWER.index((i, j)) * 8
-    return jnp.concatenate([g_ref[chip, first : first + 8, :] for chip in range(BLOCK // 8)], axis=0)
-
-
-def chol_solve(parts, x):
+def lower_block(core, own_ref, other_ref, i, j):
+    half, slot = divmod(LOWER.index((i, j)), len(LOWER) // 2)
+    mine = jnp.broadcast_to(core, (8, BLOCK)) == half
+    at = slice(slot * 8, slot * 8 + 8)
+    parts = [jnp.where(mine, own_ref[chip, at, :], other_ref[chip, at, :]) for chip in range(BLOCK // 8)]
+    return jnp.concatenate(parts, axis=0)
+
+
+def chol_solve(core, own, other, x):
     rows, n = x.shape
     return pl.pallas_call(
         chol_kernel,
         out_shape=(jax.ShapeDtypeStruct((n, n), jnp.float32), jax.ShapeDtypeStruct(x.shape, jnp.float32)),
-        in_specs=[VMEM, VMEM],
+        in_specs=[SMEM, VMEM, VMEM, VMEM],
         out_specs=[pl.BlockSpec(memory_space=pl.ANY)] * 2,
         scratch_shapes=[
             pltpu.VMEM((n, n), jnp.float32),
@@ -173,7 +176,7 @@
             pltpu.SemaphoreType.DMA((2 * (n // BLOCK),)),
         ],
         compiler_params=PARAMS,
-    )(parts, x)
+    )(core.reshape(1), own, other, x)
 
 
 def gram_kernel(chip_ref, p_ref, o_ref):
@@ -241,13 +244,12 @@
     return (1 - 2 * (v & 1)).astype(jnp.float32)
 
 
-def mix_kernel(pos_ref, x_ref, samples_ref, o_ref, h_ref):
-    width = x_ref.shape[0]
-    depth = x_ref.shape[1]
-    sources = 32
+def mix_kernel(place_ref, x_ref, samples_ref, o_ref, h_ref):
+    width, depth = x_ref.shape
+    sources = 16
     cols = width // sources
     hi, lo = split2(x_ref[...])
-    z_bits = pos_ref[0]
+    mask = place_ref[0] * 16 + place_ref[1]
     scale = 1.0 / 512.0
     for c in range(samples_ref.shape[1] // CHUNK):
         s = samples_ref[:, c * CHUNK : (c + 1) * CHUNK]
@@ -257,33 +259,33 @@
         high = signs_of(within // 16, depth // 16)
         for r in range(depth // 16):
             h_ref[r * 16 : (r + 1) * 16, :] = (low * high[r : r + 1, :]).astype(jnp.bfloat16)
-        plane_sign = signs_of((device & 15) | ((device // 256) * 16), sources)
-        zv = (device // 16) & z_bits
-        zv = zv ^ (zv >> 2)
-        zv = zv ^ (zv >> 1)
-        z_sign = (1 - 2 * (zv & 1)).astype(jnp.float32) * scale
+        chip_sign = signs_of(((device // 2) & 7) | ((device // 256) * 8), sources)
+        v = device & mask
+        for shift in (4, 2, 1):
+            v = v ^ (v >> shift)
+        own_sign = (1 - 2 * (v & 1)).astype(jnp.float32) * scale
         h = h_ref[...]
         t = jnp.dot(hi, h, preferred_element_type=jnp.float32)
         t = t + jnp.dot(lo, h, preferred_element_type=jnp.float32)
         acc = t[:cols, :]
         for p in range(1, sources):
-            acc = acc + t[p * cols : (p + 1) * cols, :] * plane_sign[p : p + 1, :]
-        acc = acc * z_sign
+            acc = acc + t[p * cols : (p + 1) * cols, :] * chip_sign[p : p + 1, :]
+        acc = acc * own_sign
         for b in range(CHUNK // SHARE):
             o_ref[c * (CHUNK // SHARE) + b] = acc[:, b * SHARE : (b + 1) * SHARE]
 
 
-def sample_columns(columns, samples, z_index):
+def sample_columns(columns, samples, place):
     width = columns.shape[0]
     count = samples.shape[0]
     return pl.pallas_call(
         mix_kernel,
-        out_shape=jax.ShapeDtypeStruct((count // SHARE, width // 32, SHARE), jnp.float32),
+        out_shape=jax.ShapeDtypeStruct((count // SHARE, width // 16, SHARE), jnp.float32),
         in_specs=[SMEM, VMEM, VMEM],
         out_specs=VMEM,
         scratch_shapes=[pltpu.VMEM((columns.shape[1], CHUNK), jnp.bfloat16)],
         compiler_params=PARAMS,
-    )(z_index.reshape(1), columns, samples.reshape(1, count))
+    )(place, columns, samples.reshape(1, count))
 
 
 def exchange(block, axes):
@@ -297,15 +299,19 @@
 
 def body(matrix, signs, samples):
     rows, n = matrix.shape
-    plane = lax.axis_size(PLANE)
-    columns = exchange(signed_columns(matrix, signs).reshape(plane, n // plane, rows), PLANE)
-    partial = sample_columns(columns.reshape(n, rows), samples, lax.axis_index(("z_hi", "z_lo")))
-    mine = exchange(partial, NEAR).reshape(lax.axis_size("z_lo"), 2 * (n // plane), -1)
-    mine = jnp.sum(gather(jnp.sum(mine, axis=0), "z_hi"), axis=0)
+    chips = lax.axis_size(CHIPS)
+    core = lax.axis_index("core")
+    columns = exchange(signed_columns(matrix, signs).reshape(chips, n // chips, rows), CHIPS)
+    place = jnp.stack([lax.axis_index(("z_hi", "z_lo")), core])
+    mine = jnp.sum(exchange(sample_columns(columns.reshape(n, rows), samples, place), NEAR), axis=0)
+    mine = jnp.sum(gather(mine, "z_hi"), axis=0)
     every = gather(mine, CHIPS).reshape(n, -1)
-    part = gram_part(every, lax.axis_index(CHIPS))
-    part = jnp.sum(gather(part, NEAR), axis=0) / jnp.float32(samples.shape[0])
-    return chol_solve(gather(part, CHIPS), matrix)
+    part = gram_part(every, lax.axis_index(CHIPS)).reshape(1, 2, 4 * len(LOWER), BLOCK)
+    part = jnp.broadcast_to(part, (lax.axis_size("z_lo"),) + part.shape[1:])
+    part = jnp.sum(exchange(part.reshape((-1,) + part.shape[2:]), NEAR), axis=0) / jnp.float32(samples.shape[0])
+    own = gather(part, CHIPS)
+    other = lax.ppermute(own, "core", [(0, 1), (1, 0)])
+    return chol_solve(core, own, other, matrix)
 
 
 def solution(mesh):

time: 129 us -> 130 us (level)
  starting transfers between devices: 14 us -> 15.8 us
  waiting for transfers between devices: 25.9 us -> 24.4 us
    ppermute x0 -> x1, starting transfers between devices: none -> 4.64 us  [body(): other = lax.ppermute(own, 'core', [(0, 1), (1, 0)])]
    all_to_all x2, starting transfers between devices: 14 us -> 11.2 us  [exchange(): return lax.all_to_all(block, axes, 0, 0, tiled=True)]
    all_to_all x2, waiting for transfers between devices: 25.9 us -> 23.3 us  [exchange(): return lax.all_to_all(block, axes, 0, 0, tiled=True)]
  transfers between devices with their start and end apart: 2 -> 3, of which waited for: 2 -> 3; matrix products, arithmetic and copies ran while one was open for 0% -> 0% of each run, Pallas kernels for 0% -> 0%
where the time goes in v5:
time: 130 us; the launch traced here: 129 us
  blocking collectives  67.2 us (52%)
  waiting for transfers between devices  24.4 us (19%)
  Pallas kernels  19.7 us (15%)
  starting transfers between devices  15.8 us (12%)
    all_to_all x4, blocking collectives, exchange(): return lax.all_to_all(block, axes, 0, 0, tiled=True)  67.2 us
    all_to_all x2, waiting for transfers between devices, exchange(): return lax.all_to_all(block, axes, 0, 0, tiled=True)  23.3 us
    pallas_call x1, Pallas kernels, chol_solve(): pl.pallas_call(chol_kernel, out_shape=(jax.ShapeDtypeStruct((n, n), jnp.f...  14 us
    all_to_all x2, starting transfers between devices, exchange(): return lax.all_to_all(block, axes, 0, 0, tiled=True)  11.2 us
    ppermute x1, starting transfers between devices, body(): other = lax.ppermute(own, 'core', [(0, 1), (1, 0)])  4.64 us
    pallas_call x1, Pallas kernels, sample_columns(): pl.pallas_call(mix_kernel, out_shape=jax.ShapeDtypeStruct((count // SHARE...  2.93 us
  transfers between devices with their start and end apart: 3, of which 3 were waited for; matrix products, arithmetic and copies ran while one was open for 0% of the time, Pallas kernels for 0%

profile of v5, /device:TPU:1, one launch (start us, length us, event | category | flops | bytes accessed | tf_op | source)
XLA Modules:
  0.0 129.0 jit_solution(10418250682061992977)
XLA Ops:
  0.6 2.5 %shard_map.50 = f32[512,512]{1,0:T(8,128)} custom-call(f32[512,512]{1,0:T(8,128)} %x_ref.3, s32[1,512]{1,0:T(1,128)} %bitcast.16), custom_call_target="tpu_custom_call" | custom-call | tf_op jit(solution)/shard_map/pallas_call | solution.py:226
  3.1 7.6 %all-to-all-start = ((f32[16,32,512]{2,1,0:T(8,128)}), f32[16,32,512]{2,1,0:T(8,128)S(1)}, u32[]{:S(2)}, u32[]{:S(2)}) async-start(f32[16,32,512]{2,1,0:T(8,128)} %bitcast.14), calls=%async_computation | async-start | bytes 2097152 | tf_op jit(solution)/shard_map/all_to_all | solution.py:292
  10.8 0.0 copy-start.1
  10.8 0.1 pad_add_fusion.place_ref
  10.8 14.1 %all-to-all-done = f32[16,32,512]{2,1,0:T(8,128)S(1)} async-done(((f32[16,32,512]{2,1,0:T(8,128)}), f32[16,32,512]{2,1,0:T(8,128)S(1)}, u32[]{:S(2)}, u32[]{:S(2)}) %all-to-all-start) | async-done | bytes 1048608 | tf_op jit(solution)/shard_map/all_to_all | solution.py:292
  25.0 0.0 copy-done.1
  25.0 2.9 %shard_map.51 = f32[8,32,256]{2,1,0:T(8,128)S(1)} custom-call(s32[2]{0:T(128)S(1)} %pad_add_fusion.place_ref, f32[512,512]{1,0:T(8,128)S(1)} %bitcast.10, s32[1,2048]{1,0:T(1,128)S(1)} %bitcast.13), custom_call_target="tpu_custom_call" | custom-call | tf_op jit(solution)/shard_map/pallas_call | solution.py:281
  27.9 18.8 %all_to_all.30 = f32[8,32,256]{2,1,0:T(8,128)S(1)} all-to-all(f32[8,32,256]{2,1,0:T(8,128)S(1)} %shard_map.51), channel_id=1, replica_groups=mesh['x_hi'=2,'z_hi'=4,'z_lo'=4,'x_lo'=2,'y'=4,'core'=2] {'z_lo','core'}, dimensions={0} | all-to-all | bytes 524288 | tf_op jit(solution)/shard_map/all_to_all | solution.py:292
  46.8 24.6 %all_to_all.31 = f32[4,32,256]{2,1,0:T(8,128)S(1)} all-to-all(f32[4,32,256]{2,1,0:T(8,128)S(1)} %broadcast_in_dim.10), channel_id=1, replica_groups=mesh['x_hi'=2,'z_hi'=4,'z_lo'=4,'x_lo'=2,'y'=4,'core'=2] {'z_hi'}, dimensions={0} | all-to-all | bytes 262144 | tf_op jit(solution)/shard_map/all_to_all | solution.py:292
  71.4 0.8 broadcast_in_dim.11
  72.3 3.6 %all-to-all-start.3 = ((f32[16,32,256]{2,1,0:T(8,128)}), f32[16,32,256]{2,1,0:T(8,128)S(1)}, u32[]{:S(2)}, u32[]{:S(2)}) async-start(f32[16,32,256]{2,1,0:T(8,128)} %broadcast_in_dim.11), calls=%async_computation.3 | async-start | bytes 1048576 | tf_op jit(solution)/shard_map/all_to_all | solution.py:292
  75.9 9.2 %all-to-all-done.3 = f32[16,32,256]{2,1,0:T(8,128)S(1)} async-done(((f32[16,32,256]{2,1,0:T(8,128)}), f32[16,32,256]{2,1,0:T(8,128)S(1)}, u32[]{:S(2)}, u32[]{:S(2)}) %all-to-all-start.3) | async-done | bytes 524320 | tf_op jit(solution)/shard_map/all_to_all | solution.py:292
  85.0 0.0 copy-start
  85.0 0.3 shard_map.52
  85.3 0.1 broadcast_in_dim.13
  85.4 13.0 %all_to_all.32 = f32[8,40,128]{2,1,0:T(8,128)S(1)} all-to-all(f32[8,40,128]{2,1,0:T(8,128)S(1)} %bitcast.15), channel_id=1, replica_groups=mesh['x_hi'=2,'z_hi'=4,'z_lo'=4,'x_lo'=2,'y'=4,'core'=2] {'z_lo','core'}, dimensions={0} | all-to-all | bytes 327680 | tf_op jit(solution)/shard_map/all_to_all | solution.py:292
  98.4 10.8 %all_to_all.33.own_ref = f32[16,40,128]{2,1,0:T(8,128)S(1)} all-to-all(f32[16,40,128]{2,1,0:T(8,128)S(1)} %broadcast_in_dim.14), channel_id=1, replica_groups=mesh['x_hi'=2,'z_hi'=4,'z_lo'=4,'x_lo'=2,'y'=4,'core'=2] {'x_hi','x_lo',..., dimensions={0} | all-to-all | bytes 655360 | tf_op jit(solution)/shard_map/all_to_all | solution.py:292
  109.2 4.6 %collective-permute-start = (f32[16,40,128]{2,1,0:T(8,128)S(1)}, f32[16,40,128]{2,1,0:T(8,128)S(1)}, u32[]{:S(2)}, u32[]{:S(2)}) collective-permute-start(f32[16,40,128]{2,1,0:T(8,128)S(1)} %all_to_all.33.own_ref), channel_id=1, source_target_pairs={{0,1},{1,0},{2,3},{3,2},{4,5},{5,4},{6,7},{7,6},{8,9},{9,8},{10,11... | collective-permute-start | bytes 983048 | tf_op jit(solution)/shard_map/ppermute | solution.py:313
  113.8 1.1 collective-permute-done.other_ref
  114.9 0.0 copy-done
  114.9 14.0 %shard_map.53 = (f32[512,512]{1,0:T(8,128)}, f32[512,512]{1,0:T(8,128)}) custom-call(s32[1]{0:T(128)} %bitcast.core_ref, f32[16,40,128]{2,1,0:T(8,128)S(1)} %all_to_all.33.own_ref, f32[16,40,128]{2,1,0:T(8,128)S(1)} %collective-permute-done.other_ref, f32[512,512]{1,0:T(8,128)S(1)} %copy-done), custom_call_target="tpu_custom_call" | custom-call | tf_op jit(solution)/shard_map/pallas_call | solution.py:164
  (6 shorter events, 0.1 us)
Async XLA Ops:
  3.1 21.8 %all-to-all-start = ((f32[16,32,512]{2,1,0:T(8,128)}), f32[16,32,512]{2,1,0:T(8,128)S(1)}, u32[]{:S(2)}, u32[]{:S(2)}) async-start(f32[16,32,512]{2,1,0:T(8,128)} %bitcast.14), calls=%async_computation | async-start | bytes 2097152 | tf_op jit(solution)/shard_map/all_to_all | solution.py:292
  10.8 14.2 %copy-start.1 = (s32[2048]{0:T(1024)S(1)}, s32[2048]{0:T(1024)}, u32[]{:S(2)}) copy-start(s32[2048]{0:T(1024)} %param.5) | copy-start | bytes 24580
  72.3 12.8 %all-to-all-start.3 = ((f32[16,32,256]{2,1,0:T(8,128)}), f32[16,32,256]{2,1,0:T(8,128)S(1)}, u32[]{:S(2)}, u32[]{:S(2)}) async-start(f32[16,32,256]{2,1,0:T(8,128)} %broadcast_in_dim.11), calls=%async_computation.3 | async-start | bytes 1048576 | tf_op jit(solution)/shard_map/all_to_all | solution.py:292
  85.0 29.8 %copy-start = (f32[512,512]{1,0:T(8,128)S(1)}, f32[512,512]{1,0:T(8,128)}, u32[]{:S(2)}) copy-start(f32[512,512]{1,0:T(8,128)} %x_ref.3) | copy-start | bytes 3145732
  109.2 5.7 %collective-permute-start = (f32[16,40,128]{2,1,0:T(8,128)S(1)}, f32[16,40,128]{2,1,0:T(8,128)S(1)}, u32[]{:S(2)}, u32[]{:S(2)}) collective-permute-start(f32[16,40,128]{2,1,0:T(8,128)S(1)} %all_to_all.33.own_ref), channel_id=1, source_target_pairs={{0,1},{1,0},{2,3},{3,2},{4,5},{5,4},{6,7},{7,6},{8,9},{9,8},{10,11... | collective-permute-start | bytes 983048 | tf_op jit(solution)/shard_map/ppermute | solution.py:313

commit v6 on v4

--- a/solution.py
+++ b/solution.py
@@ -90,7 +90,19 @@
                 v = v - low[j, i] * back[j]
                 w = w - low[j, i + 1] * back[j]
             back[i], back[i + 1] = v, w
-        for r in range(k + 1, groups):
+        if k + 1 < groups:
+            part, near = jnp.where(own, 0.0, rows[k + 1]), []
+            for i in range(8):
+                u = jnp.broadcast_to(rows[k + 1][:, base + i : base + i + 1], full)
+                for j in range(i - i % 2):
+                    u = u - low[i, j] * near[j]
+                near.append(u)
+            for i in range(0, 8, 2):
+                x, y, z = inv[i]
+                v, w = fwd[i] * x - fwd[i + 1] * y, fwd[i + 1] * z - fwd[i] * y
+                part = part - (near[i] * v + near[i + 1] * w)
+            rows[k + 1] = part
+        for r in range(k + 2, groups):
             terms = [jnp.broadcast_to(rows[r][:, base + j : base + j + 1], full) * back[j] for j in range(8)]
             while len(terms) > 1:
                 terms = [x + y for x, y in zip(terms[::2], terms[1::2])]
@@ -103,7 +115,7 @@
             w_ref[base + g : base + g + 1, :] = jnp.where(lane <= base + g, w * root[g], 0.0)[:1, :]
 
 
-def chol_kernel(g_ref, x_ref, l_out, o_out, a_ref, l_ref, o_ref, c_ref, u_ref, w_ref, sems):
+def chol_kernel(core_ref, own_ref, other_ref, x_ref, l_out, o_out, a_ref, l_ref, o_ref, c_ref, u_ref, w_ref, sems):
     n = x_ref.shape[1]
     nb = n // BLOCK
     at = [slice(k * BLOCK, (k + 1) * BLOCK) for k in range(nb)]
@@ -111,8 +123,9 @@
     c = lax.broadcasted_iota(jnp.int32, (BLOCK, BLOCK), 1)
     row_scale, col_scale, row_root = [], [], []
     copies = []
+    gram = lambda i, j: lower_block(core_ref[0], own_ref, other_ref, i, j)
     for k in range(nb):
-        diag = jnp.where(r == c, lower_block(g_ref, k, k), 0.0)
+        diag = jnp.where(r == c, gram(k, k), 0.0)
         by_row = jnp.broadcast_to(jnp.sum(diag, axis=1, keepdims=True), (BLOCK, BLOCK))
         s = lax.rsqrt(by_row)
         row_scale.append(s)
@@ -120,7 +133,7 @@
         col_scale.append(lax.rsqrt(jnp.sum(diag, axis=0, keepdims=True)))
     for k in range(nb):
         for i in range(k, nb):
-            a_ref[at[i], at[k]] = lower_block(g_ref, i, k) * row_scale[i] * col_scale[k]
+            a_ref[at[i], at[k]] = gram(i, k) * row_scale[i] * col_scale[k]
     for k in range(nb):
         panels = [a_ref[k * BLOCK + p * 8 : k * BLOCK + (p + 1) * 8, at[k]] for p in range(BLOCK // 8)]
         factor_block(panels, c_ref, u_ref.at[k % 2], w_ref.at[k % 2])
@@ -151,17 +164,20 @@
         copy.wait()
 
 
-def lower_block(g_ref, i, j):
-    first = LOWER.index((i, j)) * 8
-    return jnp.concatenate([g_ref[chip, first : first + 8, :] for chip in range(BLOCK // 8)], axis=0)
-
-
-def chol_solve(parts, x):
+def lower_block(core, own_ref, other_ref, i, j):
+    half, slot = divmod(LOWER.index((i, j)), len(LOWER) // 2)
+    mine = jnp.broadcast_to(core, (8, BLOCK)) == half
+    at = slice(slot * 8, slot * 8 + 8)
+    parts = [jnp.where(mine, own_ref[chip, at, :], other_ref[chip, at, :]) for chip in range(BLOCK // 8)]
+    return jnp.concatenate(parts, axis=0)
+
+
+def chol_solve(core, own, other, x):
     rows, n = x.shape
     return pl.pallas_call(
         chol_kernel,
         out_shape=(jax.ShapeDtypeStruct((n, n), jnp.float32), jax.ShapeDtypeStruct(x.shape, jnp.float32)),
-        in_specs=[VMEM, VMEM],
+        in_specs=[SMEM, VMEM, VMEM, VMEM],
         out_specs=[pl.BlockSpec(memory_space=pl.ANY)] * 2,
         scratch_shapes=[
             pltpu.VMEM((n, n), jnp.float32),
@@ -173,7 +189,7 @@
             pltpu.SemaphoreType.DMA((2 * (n // BLOCK),)),
         ],
         compiler_params=PARAMS,
-    )(parts, x)
+    )(core.reshape(1), own, other, x)
 
 
 def gram_kernel(chip_ref, p_ref, o_ref):
@@ -286,6 +302,22 @@
     )(z_index.reshape(1), columns, samples.reshape(1, count))
 
 
+def fan_kernel(x_ref, o_ref):
+    total = jnp.sum(x_ref[...], axis=0)
+    for i in range(o_ref.shape[0]):
+        o_ref[i] = total
+
+
+def fan_out(blocks, count):
+    return pl.pallas_call(
+        fan_kernel,
+        out_shape=jax.ShapeDtypeStruct((count,) + blocks.shape[1:], jnp.float32),
+        in_specs=[VMEM],
+        out_specs=VMEM,
+        compiler_params=PARAMS,
+    )(blocks)
+
+
 def exchange(block, axes):
     return lax.all_to_all(block, axes, 0, 0, tiled=True)
 
@@ -298,14 +330,18 @@
 def body(matrix, signs, samples):
     rows, n = matrix.shape
     plane = lax.axis_size(PLANE)
+    core = lax.axis_index("core")
     columns = exchange(signed_columns(matrix, signs).reshape(plane, n // plane, rows), PLANE)
     partial = sample_columns(columns.reshape(n, rows), samples, lax.axis_index(("z_hi", "z_lo")))
     mine = exchange(partial, NEAR).reshape(lax.axis_size("z_lo"), 2 * (n // plane), -1)
-    mine = jnp.sum(gather(jnp.sum(mine, axis=0), "z_hi"), axis=0)
-    every = gather(mine, CHIPS).reshape(n, -1)
-    part = gram_part(every, lax.axis_index(CHIPS))
-    part = jnp.sum(gather(part, NEAR), axis=0) / jnp.float32(samples.shape[0])
-    return chol_solve(gather(part, CHIPS), matrix)
+    mine = fan_out(gather(jnp.sum(mine, axis=0), "z_hi"), lax.axis_size(CHIPS))
+    every = exchange(mine, CHIPS).reshape(n, -1)
+    part = gram_part(every, lax.axis_index(CHIPS)).reshape(1, 2, 4 * len(LOWER), BLOCK)
+    part = jnp.broadcast_to(part, (lax.axis_size("z_lo"),) + part.shape[1:])
+    part = jnp.sum(exchange(part.reshape((-1,) + part.shape[2:]), NEAR), axis=0) / jnp.float32(samples.shape[0])
+    own = gather(part, CHIPS)
+    other = lax.ppermute(own, "core", [(0, 1), (1, 0)])
+    return chol_solve(core, own, other, matrix)
 
 
 def solution(mesh):

time: 129 us -> 126 us (0.977)
  blocking collectives: 67.4 us -> 59 us
  starting transfers between devices: 14 us -> 18.7 us
    all_to_all x4, blocking collectives: 67.4 us -> 59 us  [exchange(): return lax.all_to_all(block, axes, 0, 0, tiled=True)]
    ppermute x0 -> x1, starting transfers between devices: none -> 4.64 us  [body(): other = lax.ppermute(own, 'core', [(0, 1), (1, 0)])]
  transfers between devices with their start and end apart: 2 -> 3, of which waited for: 2 -> 3; matrix products, arithmetic and copies ran while one was open for 0% -> 0% of each run, Pallas kernels for 0% -> 0%
where the time goes in v6:
time: 126 us; the launch traced here: 125 us
  blocking collectives  59 us (47%)
  waiting for transfers between devices  26.9 us (21%)
  Pallas kernels  19.7 us (16%)
  starting transfers between devices  18.7 us (15%)
    all_to_all x4, blocking collectives, exchange(): return lax.all_to_all(block, axes, 0, 0, tiled=True)  59 us
    all_to_all x2, waiting for transfers between devices, exchange(): return lax.all_to_all(block, axes, 0, 0, tiled=True)  25.9 us
    all_to_all x2, starting transfers between devices, exchange(): return lax.all_to_all(block, axes, 0, 0, tiled=True)  14 us
    pallas_call x1, Pallas kernels, chol_solve(): pl.pallas_call(chol_kernel, out_shape=(jax.ShapeDtypeStruct((n, n), jnp.f...  13.7 us
    ppermute x1, starting transfers between devices, body(): other = lax.ppermute(own, 'core', [(0, 1), (1, 0)])  4.64 us
  transfers between devices with their start and end apart: 3, of which 3 were waited for; matrix products, arithmetic and copies ran while one was open for 0% of the time, Pallas kernels for 0%

profile of v6, /device:TPU:1, one launch (start us, length us, event | category | flops | bytes accessed | tf_op | source)
XLA Modules:
  0.0 125.4 jit_solution(7849783700049175253)
XLA Ops:
  0.6 2.5 %shard_map.50 = f32[512,512]{1,0:T(8,128)} custom-call(f32[512,512]{1,0:T(8,128)} %x_ref.3, s32[1,512]{1,0:T(1,128)} %bitcast.20), custom_call_target="tpu_custom_call" | custom-call | tf_op jit(solution)/shard_map/pallas_call | solution.py:239
  3.1 10.5 %all-to-all-start = ((f32[32,16,512]{2,1,0:T(8,128)}), f32[32,16,512]{2,1,0:T(8,128)S(1)}, u32[]{:S(2)}, u32[]{:S(2)}) async-start(f32[32,16,512]{2,1,0:T(8,128)} %bitcast.17), calls=%async_computation | async-start | bytes 2097152 | tf_op jit(solution)/shard_map/all_to_all | solution.py:322
  13.6 0.0 copy-start.1
  13.6 17.0 %all-to-all-done = f32[32,16,512]{2,1,0:T(8,128)S(1)} async-done(((f32[32,16,512]{2,1,0:T(8,128)}), f32[32,16,512]{2,1,0:T(8,128)S(1)}, u32[]{:S(2)}, u32[]{:S(2)}) %all-to-all-start) | async-done | bytes 1048608 | tf_op jit(solution)/shard_map/all_to_all | solution.py:322
  30.6 0.0 copy-done.1
  30.6 2.4 %shard_map.51 = f32[8,16,256]{2,1,0:T(8,128)S(1)} custom-call(s32[1]{0:T(128)} %bitcast.2.pos_ref, f32[512,512]{1,0:T(8,128)S(1)} %bitcast.13, s32[1,2048]{1,0:T(1,128)S(1)} %bitcast.16), custom_call_target="tpu_custom_call" | custom-call | tf_op jit(solution)/shard_map/pallas_call | solution.py:295
  33.1 9.7 %all_to_all.30 = f32[8,16,256]{2,1,0:T(8,128)S(1)} all-to-all(f32[8,16,256]{2,1,0:T(8,128)S(1)} %shard_map.51), channel_id=1, replica_groups=mesh['x_hi'=2,'z_hi'=4,'z_lo'=4,'x_lo'=2,'y'=4,'core'=2] {'z_lo','core'}, dimensions={0} | all-to-all | bytes 262144 | tf_op jit(solution)/shard_map/all_to_all | solution.py:322
  42.8 24.7 %all_to_all.31.x_ref = f32[4,32,256]{2,1,0:T(8,128)S(1)} all-to-all(f32[4,32,256]{2,1,0:T(8,128)S(1)} %broadcast_in_dim.8), channel_id=1, replica_groups=mesh['x_hi'=2,'z_hi'=4,'z_lo'=4,'x_lo'=2,'y'=4,'core'=2] {'z_hi'}, dimensions={0} | all-to-all | bytes 262144 | tf_op jit(solution)/shard_map/all_to_all | solution.py:322
  67.5 0.9 shard_map.52
  68.3 3.6 %all-to-all-start.3 = ((f32[16,32,256]{2,1,0:T(8,128)}), f32[16,32,256]{2,1,0:T(8,128)S(1)}, u32[]{:S(2)}, u32[]{:S(2)}) async-start(f32[16,32,256]{2,1,0:T(8,128)} %shard_map.52), calls=%async_computation.3 | async-start | bytes 1048576 | tf_op jit(solution)/shard_map/all_to_all | solution.py:322
  71.9 8.9 %all-to-all-done.3 = f32[16,32,256]{2,1,0:T(8,128)S(1)} async-done(((f32[16,32,256]{2,1,0:T(8,128)}), f32[16,32,256]{2,1,0:T(8,128)S(1)}, u32[]{:S(2)}, u32[]{:S(2)}) %all-to-all-start.3) | async-done | bytes 524320 | tf_op jit(solution)/shard_map/all_to_all | solution.py:322
  80.8 0.0 copy-start
  80.8 0.3 shard_map.53
  81.1 0.1 broadcast_in_dim.10
  81.2 13.9 %all_to_all.32 = f32[8,40,128]{2,1,0:T(8,128)S(1)} all-to-all(f32[8,40,128]{2,1,0:T(8,128)S(1)} %bitcast.18), channel_id=1, replica_groups=mesh['x_hi'=2,'z_hi'=4,'z_lo'=4,'x_lo'=2,'y'=4,'core'=2] {'z_lo','core'}, dimensions={0} | all-to-all | bytes 327680 | tf_op jit(solution)/shard_map/all_to_all | solution.py:322
  95.2 10.8 %all_to_all.33.own_ref = f32[16,40,128]{2,1,0:T(8,128)S(1)} all-to-all(f32[16,40,128]{2,1,0:T(8,128)S(1)} %broadcast_in_dim.22), channel_id=1, replica_groups=mesh['x_hi'=2,'z_hi'=4,'z_lo'=4,'x_lo'=2,'y'=4,'core'=2] {'x_hi','x_lo',..., dimensions={0} | all-to-all | bytes 655360 | tf_op jit(solution)/shard_map/all_to_all | solution.py:322
  105.9 4.6 %collective-permute-start = (f32[16,40,128]{2,1,0:T(8,128)S(1)}, f32[16,40,128]{2,1,0:T(8,128)S(1)}, u32[]{:S(2)}, u32[]{:S(2)}) collective-permute-start(f32[16,40,128]{2,1,0:T(8,128)S(1)} %all_to_all.33.own_ref), channel_id=1, source_target_pairs={{0,1},{1,0},{2,3},{3,2},{4,5},{5,4},{6,7},{7,6},{8,9},{9,8},{10,11... | collective-permute-start | bytes 983048 | tf_op jit(solution)/shard_map/ppermute | solution.py:343
  110.6 1.0 collective-permute-done.other_ref
  111.6 0.0 copy-done
  111.6 13.7 %shard_map.54 = (f32[512,512]{1,0:T(8,128)}, f32[512,512]{1,0:T(8,128)}) custom-call(s32[1]{0:T(128)} %bitcast.core_ref, f32[16,40,128]{2,1,0:T(8,128)S(1)} %all_to_all.33.own_ref, f32[16,40,128]{2,1,0:T(8,128)S(1)} %collective-permute-done.other_ref, f32[512,512]{1,0:T(8,128)S(1)} %copy-done), custom_call_target="tpu_custom_call" | custom-call | tf_op jit(solution)/shard_map/pallas_call | solution.py:177
  (5 shorter events, 0.1 us)
Async XLA Ops:
  3.1 27.5 %all-to-all-start = ((f32[32,16,512]{2,1,0:T(8,128)}), f32[32,16,512]{2,1,0:T(8,128)S(1)}, u32[]{:S(2)}, u32[]{:S(2)}) async-start(f32[32,16,512]{2,1,0:T(8,128)} %bitcast.17), calls=%async_computation | async-start | bytes 2097152 | tf_op jit(solution)/shard_map/all_to_all | solution.py:322
  13.6 17.0 %copy-start.1 = (s32[2048]{0:T(1024)S(1)}, s32[2048]{0:T(1024)}, u32[]{:S(2)}) copy-start(s32[2048]{0:T(1024)} %param.5) | copy-start | bytes 24580
  68.3 12.5 %all-to-all-start.3 = ((f32[16,32,256]{2,1,0:T(8,128)}), f32[16,32,256]{2,1,0:T(8,128)S(1)}, u32[]{:S(2)}, u32[]{:S(2)}) async-start(f32[16,32,256]{2,1,0:T(8,128)} %shard_map.52), calls=%async_computation.3 | async-start | bytes 1048576 | tf_op jit(solution)/shard_map/all_to_all | solution.py:322
  80.8 30.8 %copy-start = (f32[512,512]{1,0:T(8,128)S(1)}, f32[512,512]{1,0:T(8,128)}, u32[]{:S(2)}) copy-start(f32[512,512]{1,0:T(8,128)} %x_ref.3) | copy-start | bytes 3145732
  105.9 5.7 %collective-permute-start = (f32[16,40,128]{2,1,0:T(8,128)S(1)}, f32[16,40,128]{2,1,0:T(8,128)S(1)}, u32[]{:S(2)}, u32[]{:S(2)}) collective-permute-start(f32[16,40,128]{2,1,0:T(8,128)S(1)} %all_to_all.33.own_ref), channel_id=1, source_target_pairs={{0,1},{1,0},{2,3},{3,2},{4,5},{5,4},{6,7},{7,6},{8,9},{9,8},{10,11... | collective-permute-start | bytes 983048 | tf_op jit(solution)/shard_map/ppermute | solution.py:343

commit v7 on v6

--- a/solution.py
+++ b/solution.py
@@ -48,10 +48,9 @@
     for k in range(groups):
         base = k * 8
         own = (lane >= base) & (lane < base + 8)
-        panel = rows[k]
         for j in range(8):
-            c_ref[k % 2, j] = jnp.broadcast_to(panel[:, base + j : base + j + 1], full)
-        c_ref[k % 2, 8] = panel
+            c_ref[k % 2, j] = jnp.broadcast_to(rows[0][:, j : j + 1], full) if k == 0 else ahead[j]
+        c_ref[k % 2, 8] = rows[k]
         spread = lambda j, i: jnp.broadcast_to(c_ref[k % 2, j, i : i + 1, :], full)
         piv = {(i, j): spread(j, i) for i in range(8) for j in range(i + 1)}
         root, inv, low, ratio = {}, {}, {}, {}
@@ -92,6 +91,7 @@
             back[i], back[i + 1] = v, w
         if k + 1 < groups:
             part, near = jnp.where(own, 0.0, rows[k + 1]), []
+            ahead = [jnp.broadcast_to(rows[k + 1][:, base + 8 + j : base + 9 + j], full) for j in range(8)]
             for i in range(8):
                 u = jnp.broadcast_to(rows[k + 1][:, base + i : base + i + 1], full)
                 for j in range(i - i % 2):
@@ -101,6 +101,10 @@
                 x, y, z = inv[i]
                 v, w = fwd[i] * x - fwd[i + 1] * y, fwd[i + 1] * z - fwd[i] * y
                 part = part - (near[i] * v + near[i + 1] * w)
+                c_ref[k % 2, 9 + i] = near[i] * x - near[i + 1] * y
+                c_ref[k % 2, 10 + i] = near[i + 1] * z - near[i] * y
+                for j in range(8):
+                    ahead[j] = ahead[j] - (near[i] * spread(9 + i, j) + near[i + 1] * spread(10 + i, j))
             rows[k + 1] = part
         for r in range(k + 2, groups):
             terms = [jnp.broadcast_to(rows[r][:, base + j : base + j + 1], full) * back[j] for j in range(8)]
@@ -183,7 +187,7 @@
             pltpu.VMEM((n, n), jnp.float32),
             pltpu.VMEM((n, n), jnp.float32),
             pltpu.VMEM((rows, n), jnp.float32),
-            pltpu.VMEM((2, 9, 8, BLOCK), jnp.float32),
+            pltpu.VMEM((2, 17, 8, BLOCK), jnp.float32),
             pltpu.VMEM((2, BLOCK, BLOCK), jnp.float32),
             pltpu.VMEM((2, BLOCK, BLOCK), jnp.float32),
             pltpu.SemaphoreType.DMA((2 * (n // BLOCK),)),
@@ -192,45 +196,55 @@
     )(core.reshape(1), own, other, x)
 
 
-def gram_kernel(chip_ref, p_ref, o_ref):
-    blocks = p_ref.shape[0] // BLOCK
+def gram_kernel(chip_ref, p_ref, o_ref, all_ref):
+    blocks = all_ref.shape[0] // BLOCK
+    half = p_ref.shape[2] // 2
+    for chip in range(p_ref.shape[0]):
+        for core in range(2):
+            all_ref[chip * 32 + core * 16 : chip * 32 + core * 16 + 16, :] = p_ref[chip, :, core * half : (core + 1) * half]
     first = chip_ref[0] * 8
-    rows = [p_ref[pl.ds(pl.multiple_of(i * BLOCK + first, 8), 8), :] for i in range(blocks)]
-    product = dot_t(left(jnp.concatenate(rows, axis=0)), right(p_ref[...]))
+    rows = [all_ref[pl.ds(pl.multiple_of(i * BLOCK + first, 8), 8), :] for i in range(blocks)]
+    product = dot_t(left(jnp.concatenate(rows, axis=0)), right(all_ref[...]))
     for t, (i, j) in enumerate(LOWER):
         o_ref[t * 8 : t * 8 + 8, :] = product[i * 8 : i * 8 + 8, j * BLOCK : (j + 1) * BLOCK]
 
 
 def gram_part(columns, chip):
+    chips, group, depth = columns.shape
     return pl.pallas_call(
         gram_kernel,
         out_shape=jax.ShapeDtypeStruct((8 * len(LOWER), BLOCK), jnp.float32),
         in_specs=[SMEM, VMEM],
         out_specs=VMEM,
+        scratch_shapes=[pltpu.VMEM((2 * chips * group, depth // 2), jnp.float32)],
         compiler_params=PARAMS,
     )(chip.reshape(1), columns)
 
 
-def flip_kernel(x_ref, signs_ref, o_ref, buf_ref, row_ref, sems):
+def flip_kernel(x_ref, signs_ref, o_ref, buf_ref, row_ref, t_ref, sems):
     rows, n = buf_ref.shape
     parts = rows // BLOCK
-    sign_copy = pltpu.make_async_copy(signs_ref, row_ref, sems.at[parts])
-    copies = []
+    sign_copy = pltpu.make_async_copy(signs_ref, row_ref, sems.at[2 * parts])
+    loads, stores = [], []
     for k in range(parts):
         at = pl.ds(k * BLOCK, BLOCK)
-        copies.append(pltpu.make_async_copy(x_ref.at[at, :], buf_ref.at[at, :], sems.at[k]))
-    copies[0].start()
+        loads.append(pltpu.make_async_copy(x_ref.at[at, :], buf_ref.at[at, :], sems.at[k]))
+        stores.append(pltpu.make_async_copy(t_ref.at[:, at], o_ref.at[:, at], sems.at[parts + k]))
+    loads[0].start()
     sign_copy.start()
-    for copy in copies[1:]:
-        copy.start()
+    for load in loads[1:]:
+        load.start()
     sign_copy.wait()
     for k in range(parts):
-        copies[k].wait()
+        loads[k].wait()
         at = slice(k * BLOCK, (k + 1) * BLOCK)
         sign = row_ref[:, at].astype(jnp.float32)
         for c in range(n // BLOCK):
             cols = slice(c * BLOCK, (c + 1) * BLOCK)
-            o_ref[cols, at] = buf_ref[at, cols].T * sign
+            t_ref[cols, at] = buf_ref[at, cols].T * sign
+        stores[k].start()
+    for store in stores:
+        store.wait()
 
 
 def signed_columns(matrix, signs):
@@ -240,11 +254,12 @@
         flip_kernel,
         out_shape=jax.ShapeDtypeStruct((n, rows), jnp.float32),
         in_specs=[hbm, hbm],
-        out_specs=VMEM,
+        out_specs=hbm,
         scratch_shapes=[
             pltpu.VMEM((rows, n), jnp.float32),
             pltpu.VMEM((1, rows), jnp.int32),
-            pltpu.SemaphoreType.DMA((rows // BLOCK + 1,)),
+            pltpu.VMEM((n, rows), jnp.float32),
+            pltpu.SemaphoreType.DMA((2 * (rows // BLOCK) + 1,)),
         ],
         compiler_params=WIDE,
     )(matrix, signs.reshape(1, -1))
@@ -302,16 +317,19 @@
     )(z_index.reshape(1), columns, samples.reshape(1, count))
 
 
-def fan_kernel(x_ref, o_ref):
-    total = jnp.sum(x_ref[...], axis=0)
-    for i in range(o_ref.shape[0]):
-        o_ref[i] = total
-
-
-def fan_out(blocks, count):
-    return pl.pallas_call(
-        fan_kernel,
-        out_shape=jax.ShapeDtypeStruct((count,) + blocks.shape[1:], jnp.float32),
+def near_kernel(x_ref, o_ref):
+    half = x_ref.shape[2]
+    for core in range(2):
+        total = x_ref[core]
+        for z in range(1, x_ref.shape[0] // 2):
+            total = total + x_ref[2 * z + core]
+        o_ref[:, core * half : (core + 1) * half] = total
+
+
+def near_sum(blocks):
+    return pl.pallas_call(
+        near_kernel,
+        out_shape=jax.ShapeDtypeStruct((blocks.shape[1], 2 * blocks.shape[2]), jnp.float32),
         in_specs=[VMEM],
         out_specs=VMEM,
         compiler_params=PARAMS,
@@ -333,9 +351,9 @@
     core = lax.axis_index("core")
     columns = exchange(signed_columns(matrix, signs).reshape(plane, n // plane, rows), PLANE)
     partial = sample_columns(columns.reshape(n, rows), samples, lax.axis_index(("z_hi", "z_lo")))
-    mine = exchange(partial, NEAR).reshape(lax.axis_size("z_lo"), 2 * (n // plane), -1)
-    mine = fan_out(gather(jnp.sum(mine, axis=0), "z_hi"), lax.axis_size(CHIPS))
-    every = exchange(mine, CHIPS).reshape(n, -1)
+    mine = near_sum(exchange(partial, NEAR))
+    mine = jnp.sum(gather(mine, "z_hi"), axis=0)
+    every = gather(mine, CHIPS)
     part = gram_part(every, lax.axis_index(CHIPS)).reshape(1, 2, 4 * len(LOWER), BLOCK)
     part = jnp.broadcast_to(part, (lax.axis_size("z_lo"),) + part.shape[1:])
     part = jnp.sum(exchange(part.reshape((-1,) + part.shape[2:]), NEAR), axis=0) / jnp.float32(samples.shape[0])

time: 126 us -> 125 us (level)
  Pallas kernels: 19.7 us -> 18.4 us
where the time goes in v7:
time: 125 us
  blocking collectives  59 us (47%)
  waiting for transfers between devices  26.9 us (22%)
  starting transfers between devices  18.7 us (15%)
  Pallas kernels  18.4 us (15%)
    all_to_all x4, blocking collectives, exchange(): return lax.all_to_all(block, axes, 0, 0, tiled=True)  59 us
    all_to_all x2, waiting for transfers between devices, exchange(): return lax.all_to_all(block, axes, 0, 0, tiled=True)  25.9 us
    all_to_all x2, starting transfers between devices, exchange(): return lax.all_to_all(block, axes, 0, 0, tiled=True)  14 us
    pallas_call x1, Pallas kernels, chol_solve(): pl.pallas_call(chol_kernel, out_shape=(jax.ShapeDtypeStruct((n, n), jnp.f...  13.4 us
    ppermute x1, starting transfers between devices, body(): other = lax.ppermute(own, 'core', [(0, 1), (1, 0)])  4.64 us
  transfers between devices with their start and end apart: 3, of which 3 were waited for; matrix products, arithmetic and copies ran while one was open for 0% of the time, Pallas kernels for 0%

profile of v7, /device:TPU:1, one launch (start us, length us, event | category | flops | bytes accessed | tf_op | source)
XLA Modules:
  0.0 125.0 jit_solution(5970860628518468999)
XLA Ops:
  0.6 2.3 %shard_map.50 = f32[512,512]{1,0:T(8,128)} custom-call(f32[512,512]{1,0:T(8,128)} %x_ref.3, s32[1,512]{1,0:T(1,128)} %bitcast.14), custom_call_target="tpu_custom_call" | custom-call | tf_op jit(solution)/shard_map/pallas_call | solution.py:253
  2.9 10.5 %all-to-all-start = ((f32[32,16,512]{2,1,0:T(8,128)}), f32[32,16,512]{2,1,0:T(8,128)S(1)}, u32[]{:S(2)}, u32[]{:S(2)}) async-start(f32[32,16,512]{2,1,0:T(8,128)} %bitcast.12), calls=%async_computation | async-start | bytes 2097152 | tf_op jit(solution)/shard_map/all_to_all | solution.py:340
  13.4 0.0 copy-start.1
  13.4 17.0 %all-to-all-done = f32[32,16,512]{2,1,0:T(8,128)S(1)} async-done(((f32[32,16,512]{2,1,0:T(8,128)}), f32[32,16,512]{2,1,0:T(8,128)S(1)}, u32[]{:S(2)}, u32[]{:S(2)}) %all-to-all-start) | async-done | bytes 1048608 | tf_op jit(solution)/shard_map/all_to_all | solution.py:340
  30.4 0.0 copy-done.1
  30.4 2.4 %shard_map.51 = f32[8,16,256]{2,1,0:T(8,128)S(1)} custom-call(s32[1]{0:T(128)} %bitcast.2.pos_ref, f32[512,512]{1,0:T(8,128)S(1)} %bitcast.9, s32[1,2048]{1,0:T(1,128)S(1)} %bitcast.11), custom_call_target="tpu_custom_call" | custom-call | tf_op jit(solution)/shard_map/pallas_call | solution.py:310
  32.8 9.7 %all_to_all.30.x_ref = f32[8,16,256]{2,1,0:T(8,128)S(1)} all-to-all(f32[8,16,256]{2,1,0:T(8,128)S(1)} %shard_map.51), channel_id=1, replica_groups=mesh['x_hi'=2,'z_hi'=4,'z_lo'=4,'x_lo'=2,'y'=4,'core'=2] {'z_lo','core'}, dimensions={0} | all-to-all | bytes 262144 | tf_op jit(solution)/shard_map/all_to_all | solution.py:340
  42.6 24.7 %all_to_all.31 = f32[4,16,512]{2,1,0:T(8,128)S(1)} all-to-all(f32[4,16,512]{2,1,0:T(8,128)S(1)} %broadcast_in_dim.10), channel_id=1, replica_groups=mesh['x_hi'=2,'z_hi'=4,'z_lo'=4,'x_lo'=2,'y'=4,'core'=2] {'z_hi'}, dimensions={0} | all-to-all | bytes 262144 | tf_op jit(solution)/shard_map/all_to_all | solution.py:340
  67.3 0.9 broadcast_in_dim.11
  68.1 3.6 %all-to-all-start.3 = ((f32[16,16,512]{2,1,0:T(8,128)}), f32[16,16,512]{2,1,0:T(8,128)S(1)}, u32[]{:S(2)}, u32[]{:S(2)}) async-start(f32[16,16,512]{2,1,0:T(8,128)} %broadcast_in_dim.11), calls=%async_computation.3 | async-start | bytes 1048576 | tf_op jit(solution)/shard_map/all_to_all | solution.py:340
  71.7 8.9 %all-to-all-done.3.p_ref = f32[16,16,512]{2,1,0:T(8,128)S(1)} async-done(((f32[16,16,512]{2,1,0:T(8,128)}), f32[16,16,512]{2,1,0:T(8,128)S(1)}, u32[]{:S(2)}, u32[]{:S(2)}) %all-to-all-start.3) | async-done | bytes 524320 | tf_op jit(solution)/shard_map/all_to_all | solution.py:340
  80.6 0.0 copy-start
  80.6 0.3 shard_map.53
  80.9 0.1 broadcast_in_dim.13
  81.0 13.9 %all_to_all.32 = f32[8,40,128]{2,1,0:T(8,128)S(1)} all-to-all(f32[8,40,128]{2,1,0:T(8,128)S(1)} %bitcast.13), channel_id=1, replica_groups=mesh['x_hi'=2,'z_hi'=4,'z_lo'=4,'x_lo'=2,'y'=4,'core'=2] {'z_lo','core'}, dimensions={0} | all-to-all | bytes 327680 | tf_op jit(solution)/shard_map/all_to_all | solution.py:340
  95.0 10.8 %all_to_all.33.own_ref = f32[16,40,128]{2,1,0:T(8,128)S(1)} all-to-all(f32[16,40,128]{2,1,0:T(8,128)S(1)} %broadcast_in_dim.14), channel_id=1, replica_groups=mesh['x_hi'=2,'z_hi'=4,'z_lo'=4,'x_lo'=2,'y'=4,'core'=2] {'x_hi','x_lo',..., dimensions={0} | all-to-all | bytes 655360 | tf_op jit(solution)/shard_map/all_to_all | solution.py:340
  105.7 4.6 %collective-permute-start = (f32[16,40,128]{2,1,0:T(8,128)S(1)}, f32[16,40,128]{2,1,0:T(8,128)S(1)}, u32[]{:S(2)}, u32[]{:S(2)}) collective-permute-start(f32[16,40,128]{2,1,0:T(8,128)S(1)} %all_to_all.33.own_ref), channel_id=1, source_target_pairs={{0,1},{1,0},{2,3},{3,2},{4,5},{5,4},{6,7},{7,6},{8,9},{9,8},{10,11... | collective-permute-start | bytes 983048 | tf_op jit(solution)/shard_map/ppermute | solution.py:361
  110.4 1.0 collective-permute-done.other_ref
  111.4 0.0 copy-done
  111.4 13.4 %shard_map.54 = (f32[512,512]{1,0:T(8,128)}, f32[512,512]{1,0:T(8,128)}) custom-call(s32[1]{0:T(128)} %bitcast.core_ref, f32[16,40,128]{2,1,0:T(8,128)S(1)} %all_to_all.33.own_ref, f32[16,40,128]{2,1,0:T(8,128)S(1)} %collective-permute-done.other_ref, f32[512,512]{1,0:T(8,128)S(1)} %copy-done), custom_call_target="tpu_custom_call" | custom-call | tf_op jit(solution)/shard_map/pallas_call | solution.py:181
  (6 shorter events, 0.1 us)
Async XLA Ops:
  2.9 27.5 %all-to-all-start = ((f32[32,16,512]{2,1,0:T(8,128)}), f32[32,16,512]{2,1,0:T(8,128)S(1)}, u32[]{:S(2)}, u32[]{:S(2)}) async-start(f32[32,16,512]{2,1,0:T(8,128)} %bitcast.12), calls=%async_computation | async-start | bytes 2097152 | tf_op jit(solution)/shard_map/all_to_all | solution.py:340
  13.4 17.0 %copy-start.1 = (s32[2048]{0:T(1024)S(1)}, s32[2048]{0:T(1024)}, u32[]{:S(2)}) copy-start(s32[2048]{0:T(1024)} %param.5) | copy-start | bytes 24580
  68.1 12.5 %all-to-all-start.3 = ((f32[16,16,512]{2,1,0:T(8,128)}), f32[16,16,512]{2,1,0:T(8,128)S(1)}, u32[]{:S(2)}, u32[]{:S(2)}) async-start(f32[16,16,512]{2,1,0:T(8,128)} %broadcast_in_dim.11), calls=%async_computation.3 | async-start | bytes 1048576 | tf_op jit(solution)/shard_map/all_to_all | solution.py:340
  80.6 30.8 %copy-start = (f32[512,512]{1,0:T(8,128)S(1)}, f32[512,512]{1,0:T(8,128)}, u32[]{:S(2)}) copy-start(f32[512,512]{1,0:T(8,128)} %x_ref.3) | copy-start | bytes 3145732
  105.7 5.7 %collective-permute-start = (f32[16,40,128]{2,1,0:T(8,128)S(1)}, f32[16,40,128]{2,1,0:T(8,128)S(1)}, u32[]{:S(2)}, u32[]{:S(2)}) collective-permute-start(f32[16,40,128]{2,1,0:T(8,128)S(1)} %all_to_all.33.own_ref), channel_id=1, source_target_pairs={{0,1},{1,0},{2,3},{3,2},{4,5},{5,4},{6,7},{7,6},{8,9},{9,8},{10,11... | collective-permute-start | bytes 983048 | tf_op jit(solution)/shard_map/ppermute | solution.py:361

commit v8 on v7

--- a/solution.py
+++ b/solution.py
@@ -106,11 +106,25 @@
                 for j in range(8):
                     ahead[j] = ahead[j] - (near[i] * spread(9 + i, j) + near[i + 1] * spread(10 + i, j))
             rows[k + 1] = part
-        for r in range(k + 2, groups):
+        far = range(min(k + 3, groups), groups) if groups - k - 3 >= 4 else ()
+        for r in range(k + 2, far[0] if far else groups):
             terms = [jnp.broadcast_to(rows[r][:, base + j : base + j + 1], full) * back[j] for j in range(8)]
             while len(terms) > 1:
                 terms = [x + y for x, y in zip(terms[::2], terms[1::2])]
             rows[r] = jnp.where(own, 0.0, rows[r]) - terms[0]
+        if far:
+            mixed = back[0]
+            for j in range(1, 8):
+                mixed = jnp.where(sub == j, back[j], mixed)
+            zero = jnp.zeros(full, jnp.float32)
+            hi, lo = split2(jnp.concatenate([zero] * k + [mixed] + [zero] * (groups - k - 1), axis=0))
+            delta = jnp.dot(
+                left(jnp.concatenate([rows[r] for r in far], axis=0)),
+                jnp.concatenate([hi, lo, hi], axis=0),
+                preferred_element_type=jnp.float32,
+            )
+            for i, r in enumerate(far):
+                rows[r] = jnp.where(own, 0.0, rows[r]) - delta[i * 8 : i * 8 + 8, :]
         for g in range(8):
             h = g - g % 2
             w = fwd[g] if g == h else fwd[g] - ratio[h] * fwd[h]
@@ -119,7 +133,7 @@
             w_ref[base + g : base + g + 1, :] = jnp.where(lane <= base + g, w * root[g], 0.0)[:1, :]
 
 
-def chol_kernel(core_ref, own_ref, other_ref, x_ref, l_out, o_out, a_ref, l_ref, o_ref, c_ref, u_ref, w_ref, sems):
+def chol_kernel(place_ref, own_ref, other_ref, x_ref, l_out, o_out, a_ref, l_ref, o_ref, c_ref, u_ref, w_ref, sems):
     n = x_ref.shape[1]
     nb = n // BLOCK
     at = [slice(k * BLOCK, (k + 1) * BLOCK) for k in range(nb)]
@@ -127,7 +141,7 @@
     c = lax.broadcasted_iota(jnp.int32, (BLOCK, BLOCK), 1)
     row_scale, col_scale, row_root = [], [], []
     copies = []
-    gram = lambda i, j: lower_block(core_ref[0], own_ref, other_ref, i, j)
+    gram = lambda i, j: lower_block(place_ref[2], own_ref, other_ref, i, j)
     for k in range(nb):
         diag = jnp.where(r == c, gram(k, k), 0.0)
         by_row = jnp.broadcast_to(jnp.sum(diag, axis=1, keepdims=True), (BLOCK, BLOCK))
@@ -176,7 +190,7 @@
     return jnp.concatenate(parts, axis=0)
 
 
-def chol_solve(core, own, other, x):
+def chol_solve(place, own, other, x):
     rows, n = x.shape
     return pl.pallas_call(
         chol_kernel,
@@ -193,23 +207,23 @@
             pltpu.SemaphoreType.DMA((2 * (n // BLOCK),)),
         ],
         compiler_params=PARAMS,
-    )(core.reshape(1), own, other, x)
-
-
-def gram_kernel(chip_ref, p_ref, o_ref, all_ref):
+    )(place, own, other, x)
+
+
+def gram_kernel(place_ref, p_ref, o_ref, all_ref):
     blocks = all_ref.shape[0] // BLOCK
     half = p_ref.shape[2] // 2
     for chip in range(p_ref.shape[0]):
         for core in range(2):
             all_ref[chip * 32 + core * 16 : chip * 32 + core * 16 + 16, :] = p_ref[chip, :, core * half : (core + 1) * half]
-    first = chip_ref[0] * 8
+    first = place_ref[1] * 8
     rows = [all_ref[pl.ds(pl.multiple_of(i * BLOCK + first, 8), 8), :] for i in range(blocks)]
     product = dot_t(left(jnp.concatenate(rows, axis=0)), right(all_ref[...]))
     for t, (i, j) in enumerate(LOWER):
         o_ref[t * 8 : t * 8 + 8, :] = product[i * 8 : i * 8 + 8, j * BLOCK : (j + 1) * BLOCK]
 
 
-def gram_part(columns, chip):
+def gram_part(columns, place):
     chips, group, depth = columns.shape
     return pl.pallas_call(
         gram_kernel,
@@ -218,7 +232,7 @@
         out_specs=VMEM,
         scratch_shapes=[pltpu.VMEM((2 * chips * group, depth // 2), jnp.float32)],
         compiler_params=PARAMS,
-    )(chip.reshape(1), columns)
+    )(place, columns)
 
 
 def flip_kernel(x_ref, signs_ref, o_ref, buf_ref, row_ref, t_ref, sems):
@@ -272,13 +286,15 @@
     return (1 - 2 * (v & 1)).astype(jnp.float32)
 
 
-def mix_kernel(pos_ref, x_ref, samples_ref, o_ref, h_ref):
+def mix_kernel(place_ref, x_ref, samples_ref, o_ref, kept_ref, h_ref):
     width = x_ref.shape[0]
     depth = x_ref.shape[1]
     sources = 32
     cols = width // sources
     hi, lo = split2(x_ref[...])
-    z_bits = pos_ref[0]
+    z_bits = place_ref[0]
+    for i in range(kept_ref.shape[0]):
+        kept_ref[i] = place_ref[i]
     scale = 1.0 / 512.0
     for c in range(samples_ref.shape[1] // CHUNK):
         s = samples_ref[:, c * CHUNK : (c + 1) * CHUNK]
@@ -304,17 +320,20 @@
             o_ref[c * (CHUNK // SHARE) + b] = acc[:, b * SHARE : (b + 1) * SHARE]
 
 
-def sample_columns(columns, samples, z_index):
+def sample_columns(columns, samples, place):
     width = columns.shape[0]
     count = samples.shape[0]
     return pl.pallas_call(
         mix_kernel,
-        out_shape=jax.ShapeDtypeStruct((count // SHARE, width // 32, SHARE), jnp.float32),
+        out_shape=(
+            jax.ShapeDtypeStruct((count // SHARE, width // 32, SHARE), jnp.float32),
+            jax.ShapeDtypeStruct(place.shape, jnp.int32),
+        ),
         in_specs=[SMEM, VMEM, VMEM],
-        out_specs=VMEM,
+        out_specs=[VMEM, SMEM],
         scratch_shapes=[pltpu.VMEM((columns.shape[1], CHUNK), jnp.bfloat16)],
         compiler_params=PARAMS,
-    )(z_index.reshape(1), columns, samples.reshape(1, count))
+    )(place, columns, samples.reshape(1, count))
 
 
 def near_kernel(x_ref, o_ref):
@@ -348,18 +367,18 @@
 def body(matrix, signs, samples):
     rows, n = matrix.shape
     plane = lax.axis_size(PLANE)
-    core = lax.axis_index("core")
+    place = jnp.stack([lax.axis_index(("z_hi", "z_lo")), lax.axis_index(CHIPS), lax.axis_index("core")])
     columns = exchange(signed_columns(matrix, signs).reshape(plane, n // plane, rows), PLANE)
-    partial = sample_columns(columns.reshape(n, rows), samples, lax.axis_index(("z_hi", "z_lo")))
+    partial, place = sample_columns(columns.reshape(n, rows), samples, place)
     mine = near_sum(exchange(partial, NEAR))
     mine = jnp.sum(gather(mine, "z_hi"), axis=0)
     every = gather(mine, CHIPS)
-    part = gram_part(every, lax.axis_index(CHIPS)).reshape(1, 2, 4 * len(LOWER), BLOCK)
+    part = gram_part(every, place).reshape(1, 2, 4 * len(LOWER), BLOCK)
     part = jnp.broadcast_to(part, (lax.axis_size("z_lo"),) + part.shape[1:])
     part = jnp.sum(exchange(part.reshape((-1,) + part.shape[2:]), NEAR), axis=0) / jnp.float32(samples.shape[0])
     own = gather(part, CHIPS)
     other = lax.ppermute(own, "core", [(0, 1), (1, 0)])
-    return chol_solve(core, own, other, matrix)
+    return chol_solve(place, own, other, matrix)
 
 
 def solution(mesh):

time: 125 us -> 126 us (level)
  blocking collectives: 59 us -> 71.3 us
  waiting for transfers between devices: 26.9 us -> 18 us
  starting transfers between devices: 18.7 us -> 15.1 us
  Pallas kernels: 18.4 us -> 19.8 us
    all_to_all x4 -> x5, blocking collectives: 59 us -> 71.3 us  [exchange(): return lax.all_to_all(block, axes, 0, 0, tiled=True)]
    all_to_all x2 -> x1, waiting for transfers between devices: 25.9 us -> 16.9 us  [exchange(): return lax.all_to_all(block, axes, 0, 0, tiled=True)]
    all_to_all x2 -> x1, starting transfers between devices: 14 us -> 10.5 us  [exchange(): return lax.all_to_all(block, axes, 0, 0, tiled=True)]
  transfers between devices with their start and end apart: 3 -> 2, of which waited for: 3 -> 2; matrix products, arithmetic and copies ran while one was open for 0% -> 0% of each run, Pallas kernels for 0% -> 0%
where the time goes in v8:
time: 126 us; the launch traced here: 125 us
  blocking collectives  71.3 us (57%)
  Pallas kernels  19.8 us (16%)
  waiting for transfers between devices  18 us (14%)
  starting transfers between devices  15.1 us (12%)
    all_to_all x5, blocking collectives, exchange(): return lax.all_to_all(block, axes, 0, 0, tiled=True)  71.3 us
    all_to_all x1, waiting for transfers between devices, exchange(): return lax.all_to_all(block, axes, 0, 0, tiled=True)  16.9 us
    pallas_call x1, Pallas kernels, chol_solve(): pl.pallas_call(chol_kernel, out_shape=(jax.ShapeDtypeStruct((n, n), jnp.f...  13.5 us
    all_to_all x1, starting transfers between devices, exchange(): return lax.all_to_all(block, axes, 0, 0, tiled=True)  10.5 us
    ppermute x1, starting transfers between devices, body(): other = lax.ppermute(own, 'core', [(0, 1), (1, 0)])  4.64 us
    pallas_call x1, Pallas kernels, sample_columns(): pl.pallas_call(mix_kernel, out_shape=(jax.ShapeDtypeStruct((count // SHAR...  3.25 us
  transfers between devices with their start and end apart: 2, of which 2 were waited for; matrix products, arithmetic and copies ran while one was open for 0% of the time, Pallas kernels for 0%

profile of v8, /device:TPU:1, one launch (start us, length us, event | category | flops | bytes accessed | tf_op | source)
XLA Modules:
  0.0 125.4 jit_solution(18425691214251247831)
XLA Ops:
  0.6 2.3 %shard_map.50 = f32[512,512]{1,0:T(8,128)} custom-call(f32[512,512]{1,0:T(8,128)} %x_ref.3, s32[1,512]{1,0:T(1,128)} %bitcast.14), custom_call_target="tpu_custom_call" | custom-call | tf_op jit(solution)/shard_map/pallas_call | solution.py:267
  2.9 10.5 %all-to-all-start = ((f32[32,16,512]{2,1,0:T(8,128)}), f32[32,16,512]{2,1,0:T(8,128)S(1)}, u32[]{:S(2)}, u32[]{:S(2)}) async-start(f32[32,16,512]{2,1,0:T(8,128)} %bitcast.12), calls=%async_computation | async-start | bytes 2097152 | tf_op jit(solution)/shard_map/all_to_all | solution.py:359
  13.4 0.0 copy-start.1
  13.4 0.1 pad_add_fusion.place_ref
  13.5 16.9 %all-to-all-done = f32[32,16,512]{2,1,0:T(8,128)S(1)} async-done(((f32[32,16,512]{2,1,0:T(8,128)}), f32[32,16,512]{2,1,0:T(8,128)S(1)}, u32[]{:S(2)}, u32[]{:S(2)}) %all-to-all-start) | async-done | bytes 1048608 | tf_op jit(solution)/shard_map/all_to_all | solution.py:359
  30.4 0.0 copy-done.1
  30.4 3.2 %shard_map.51 = (f32[8,16,256]{2,1,0:T(8,128)S(1)}, s32[3]{0:T(128)S(1)}) custom-call(s32[3]{0:T(128)S(1)} %pad_add_fusion.place_ref, f32[512,512]{1,0:T(8,128)S(1)} %bitcast.9, s32[1,2048]{1,0:T(1,128)S(1)} %bitcast.11), custom_call_target="tpu_custom_call" | custom-call | tf_op jit(solution)/shard_map/pallas_call | solution.py:326
  33.7 9.7 %all_to_all.30.x_ref = f32[8,16,256]{2,1,0:T(8,128)S(1)} all-to-all(f32[8,16,256]{2,1,0:T(8,128)S(1)} %get-tuple-element.5), channel_id=1, replica_groups=mesh['x_hi'=2,'z_hi'=4,'z_lo'=4,'x_lo'=2,'y'=4,'core'=2] {'z_lo','core'}, dimensions={0} | all-to-all | bytes 262144 | tf_op jit(solution)/shard_map/all_to_all | solution.py:359
  43.4 24.7 %all_to_all.31 = f32[4,16,512]{2,1,0:T(8,128)S(1)} all-to-all(f32[4,16,512]{2,1,0:T(8,128)S(1)} %broadcast_in_dim.10), channel_id=1, replica_groups=mesh['x_hi'=2,'z_hi'=4,'z_lo'=4,'x_lo'=2,'y'=4,'core'=2] {'z_hi'}, dimensions={0} | all-to-all | bytes 262144 | tf_op jit(solution)/shard_map/all_to_all | solution.py:359
  68.1 0.1 broadcast_in_dim.11
  68.1 12.2 %all_to_all.32.p_ref = f32[16,16,512]{2,1,0:T(8,128)S(1)} all-to-all(f32[16,16,512]{2,1,0:T(8,128)S(1)} %broadcast_in_dim.11), channel_id=1, replica_groups=mesh['x_hi'=2,'z_hi'=4,'z_lo'=4,'x_lo'=2,'y'=4,'core'=2] {'x_hi','x_lo',..., dimensions={0} | all-to-all | bytes 1048576 | tf_op jit(solution)/shard_map/all_to_all | solution.py:359
  80.4 0.0 copy-start
  80.4 0.8 shard_map.53
  81.2 0.1 broadcast_in_dim.13
  81.3 14.0 %all_to_all.33 = f32[8,40,128]{2,1,0:T(8,128)S(1)} all-to-all(f32[8,40,128]{2,1,0:T(8,128)S(1)} %bitcast.13), channel_id=1, replica_groups=mesh['x_hi'=2,'z_hi'=4,'z_lo'=4,'x_lo'=2,'y'=4,'core'=2] {'z_lo','core'}, dimensions={0} | all-to-all | bytes 327680 | tf_op jit(solution)/shard_map/all_to_all | solution.py:359
  95.3 10.8 %all_to_all.34.own_ref = f32[16,40,128]{2,1,0:T(8,128)S(1)} all-to-all(f32[16,40,128]{2,1,0:T(8,128)S(1)} %broadcast_in_dim.14), channel_id=1, replica_groups=mesh['x_hi'=2,'z_hi'=4,'z_lo'=4,'x_lo'=2,'y'=4,'core'=2] {'x_hi','x_lo',..., dimensions={0} | all-to-all | bytes 655360 | tf_op jit(solution)/shard_map/all_to_all | solution.py:359
  106.1 4.6 %collective-permute-start = (f32[16,40,128]{2,1,0:T(8,128)S(1)}, f32[16,40,128]{2,1,0:T(8,128)S(1)}, u32[]{:S(2)}, u32[]{:S(2)}) collective-permute-start(f32[16,40,128]{2,1,0:T(8,128)S(1)} %all_to_all.34.own_ref), channel_id=1, source_target_pairs={{0,1},{1,0},{2,3},{3,2},{4,5},{5,4},{6,7},{7,6},{8,9},{9,8},{10,11... | collective-permute-start | bytes 983048 | tf_op jit(solution)/shard_map/ppermute | solution.py:380
  110.7 1.1 collective-permute-done.other_ref
  111.8 0.0 copy-done
  111.8 13.5 %shard_map.54 = (f32[512,512]{1,0:T(8,128)}, f32[512,512]{1,0:T(8,128)}) custom-call(s32[3]{0:T(128)S(1)} %get-tuple-element.4.place_ref, f32[16,40,128]{2,1,0:T(8,128)S(1)} %all_to_all.34.own_ref, f32[16,40,128]{2,1,0:T(8,128)S(1)} %collective-permute-done.other_ref, f32[512,512]{1,0:T(8,128)S(1)} %copy-done), custom_call_target="tpu_custom_call" | custom-call | tf_op jit(solution)/shard_map/pallas_call | solution.py:195
  (6 shorter events, 0.1 us)
Async XLA Ops:
  2.9 27.5 %all-to-all-start = ((f32[32,16,512]{2,1,0:T(8,128)}), f32[32,16,512]{2,1,0:T(8,128)S(1)}, u32[]{:S(2)}, u32[]{:S(2)}) async-start(f32[32,16,512]{2,1,0:T(8,128)} %bitcast.12), calls=%async_computation | async-start | bytes 2097152 | tf_op jit(solution)/shard_map/all_to_all | solution.py:359
  13.4 17.0 %copy-start.1 = (s32[2048]{0:T(1024)S(1)}, s32[2048]{0:T(1024)}, u32[]{:S(2)}) copy-start(s32[2048]{0:T(1024)} %param.5) | copy-start | bytes 24580
  80.4 31.4 %copy-start = (f32[512,512]{1,0:T(8,128)S(1)}, f32[512,512]{1,0:T(8,128)}, u32[]{:S(2)}) copy-start(f32[512,512]{1,0:T(8,128)} %x_ref.3) | copy-start | bytes 3145732
  106.1 5.7 %collective-permute-start = (f32[16,40,128]{2,1,0:T(8,128)S(1)}, f32[16,40,128]{2,1,0:T(8,128)S(1)}, u32[]{:S(2)}, u32[]{:S(2)}) collective-permute-start(f32[16,40,128]{2,1,0:T(8,128)S(1)} %all_to_all.34.own_ref), channel_id=1, source_target_pairs={{0,1},{1,0},{2,3},{3,2},{4,5},{5,4},{6,7},{7,6},{8,9},{9,8},{10,11... | collective-permute-start | bytes 983048 | tf_op jit(solution)/shard_map/ppermute | solution.py:380
